TPU v7x, 128 devices: a whole 4x4x4 slice. The times are simulated.
128 devices in a mesh: seq: 2 (over x_lo), shard: 64 (over z, y, x_hi, core).
Axes of the slice: x: 4 (x_hi: 2, x_lo: 2; x = x_hi * 2 + x_lo), y: 4, z: 4, core: 2. Of those that a mesh axis runs over, the one named last changes fastest.
Arguments:
- tokens: bfloat16 [64, 2, 128, 768], P('shard', 'seq'), may hold values from -16 to 16
- cotangent: bfloat16 [64, 2, 128, 768], P('shard', 'seq'), may hold values from -6 to 6
- first_gain: bfloat16 [768], P('shard'), may hold values from 0.25 to 1.75
- first_offset: bfloat16 [768], P('shard'), may hold values from -1.75 to 1.75
- in_weight: bfloat16 [768, 2304], P('shard'), may hold values from -0.21875 to 0.21875
- query_bias: bfloat16 [768], P('shard'), may hold values from -1.75 to 1.75
- value_bias: bfloat16 [768], P('shard'), may hold values from -1.75 to 1.75
- out_weight: bfloat16 [768, 768], P('shard'), may hold values from -1.75 to 1.75
- out_bias: bfloat16 [768], P('shard'), may hold values from -1.75 to 1.75
- second_gain: bfloat16 [768], P('shard'), may hold values from 0.25 to 1.75
- second_offset: bfloat16 [768], P('shard'), may hold values from -1.75 to 1.75
- up_weight: bfloat16 [768, 3072], P('shard'), may hold values from -0.21875 to 0.21875
- up_bias: bfloat16 [3072], P('shard'), may hold values from -1.75 to 1.75
- down_weight: bfloat16 [3072, 768], P('shard'), may hold values from -0.109375 to 0.109375
- down_bias: bfloat16 [768], P('shard'), may hold values from -1.75 to 1.75
Outputs:
- layer_out: bfloat16 [64, 2, 128, 768], P('shard', 'seq')
- grad_tokens: bfloat16 [64, 2, 128, 768], P('shard', 'seq')
- grad_first_gain: float32 [768], P('shard')
- grad_first_offset: float32 [768], P('shard')
- grad_in_weight: float32 [768, 2304], P('shard')
- grad_query_bias: float32 [768], P('shard')
- grad_value_bias: float32 [768], P('shard')
- grad_out_weight: float32 [768, 768], P('shard')
- grad_out_bias: float32 [768], P('shard')
- grad_second_gain: float32 [768], P('shard')
- grad_second_offset: float32 [768], P('shard')
- grad_up_weight: float32 [768, 3072], P('shard')
- grad_up_bias: float32 [3072], P('shard')
- grad_down_weight: float32 [3072, 768], P('shard')
- grad_down_bias: float32 [768], P('shard')
All inputs are finite; a program needn't handle non-finite values.
Results may differ from a plain program's by a relative error of at most 0.025.
Values may be sent and summed in bfloat16 or wider, within the bound.
No kernel may reach another device: no remote copies, remote signals or barrier semaphores. Data moves between devices by JAX's collectives and lax.ppermute only.
A program may use at most 128 MiB of HBM per device.

v0:
```python
import jax
import jax.numpy as jnp
from jax import lax
from jax.sharding import PartitionSpec as P

HEAD_DIM = 64
SPAN = 4


def passed_along(value, axis, steps):
    count = lax.axis_size(axis)
    initial, last = (max(0, -steps), min(count, count - steps))
    return lax.ppermute(value, axis, [(source, source + steps) for source in range(initial, last)])


def gelu_tanh(inputs):
    return (
        0.5
        * inputs
        * (1.0 + jnp.tanh(0.7978845608028654 * (inputs + 0.044715 * inputs * inputs * inputs)))
    )


def layer_norm(values, norm_gain, offset):
    average = jnp.mean(values, axis=-1, keepdims=True)
    centered = values - average
    inverse = lax.rsqrt(jnp.mean(centered * centered, axis=-1, keepdims=True) + 1e-05)
    normed = centered * inverse
    return (normed * norm_gain + offset, normed, inverse)


def norm_backward(upstream, normed, inverse, norm_gain):
    scaled = upstream * norm_gain
    return inverse * (
        scaled
        - jnp.mean(scaled, axis=-1, keepdims=True)
        - normed * jnp.mean(scaled * normed, axis=-1, keepdims=True)
    )


def allowed_keys(first_row, block_rows, key_total, row_count, position):
    query_pos = first_row + lax.broadcasted_iota(jnp.int32, (block_rows, key_total), 0)
    key_index = lax.broadcasted_iota(jnp.int32, (block_rows, key_total), 1)
    key_block = key_index // row_count
    key_local = key_index % row_count
    return jnp.where(key_block == 0, key_local <= query_pos, key_block <= position)


def block_scores(queries, first_row, key_heads, row_count, position, factor):
    scores = (
        jnp.einsum("qhd,khd->hqk", queries, key_heads, preferred_element_type=jnp.float32) * factor
    )
    visible = allowed_keys(first_row, queries.shape[0], key_heads.shape[0], row_count, position)
    return jnp.where(visible[None], scores, -1e30)


def attend_block(queries, first_row, key_heads, value_heads, row_count, position, factor):
    scores = block_scores(queries, first_row, key_heads, row_count, position, factor)
    highest = jnp.max(scores, axis=-1, keepdims=True)
    exponent = jnp.exp(scores - highest)
    row_total = jnp.sum(exponent, axis=-1, keepdims=True)
    weights = (exponent / row_total).astype(jnp.bfloat16)
    output = jnp.einsum("hqk,khd->qhd", weights, value_heads, preferred_element_type=jnp.float32)
    return (output, (highest + jnp.log(row_total))[..., 0])


def attend_back(
    queries,
    grad_out,
    attended,
    log_total,
    first_row,
    key_heads,
    value_heads,
    row_count,
    position,
    factor,
):
    scores = block_scores(queries, first_row, key_heads, row_count, position, factor)
    attention = jnp.exp(scores - log_total[..., None])
    grad_probs = jnp.einsum(
        "qhd,khd->hqk", grad_out, value_heads, preferred_element_type=jnp.float32
    )
    row_inner = jnp.transpose(jnp.sum(grad_out.astype(jnp.float32) * attended, axis=-1))
    grad_scores = (attention * (grad_probs - row_inner[..., None])).astype(jnp.bfloat16)
    grad_query = (
        jnp.einsum("hqk,khd->qhd", grad_scores, key_heads, preferred_element_type=jnp.float32)
        * factor
    )
    grad_key = (
        jnp.einsum("hqk,qhd->khd", grad_scores, queries, preferred_element_type=jnp.float32)
        * factor
    )
    grad_value = jnp.einsum(
        "hqk,qhd->khd", attention.astype(jnp.bfloat16), grad_out, preferred_element_type=jnp.float32
    )
    return (grad_query, grad_key, grad_value)


def local(
    tokens,
    cotangent,
    first_gain,
    first_offset,
    in_weight,
    query_bias,
    value_bias,
    out_weight,
    out_bias,
    second_gain,
    second_offset,
    up_weight,
    up_bias,
    down_weight,
    down_bias,
):
    floating = jnp.float32
    halfwidth = jnp.bfloat16
    tok_dev = tokens.shape[2]
    width = tokens.shape[3]
    seq_count = lax.axis_size("seq")
    row_count = seq_count * tok_dev
    head_width = width // seq_count
    head_count = head_width // HEAD_DIM
    factor = HEAD_DIM ** (-0.5)
    position = lax.axis_index("shard") % SPAN
    (
        gain_one,
        offset_one,
        weight_in,
        bias_query,
        bias_value,
        weight_out,
        bias_out,
        gain_two,
        offset_two,
        weight_up,
        bias_up,
        weight_down,
        bias_down,
    ) = (
        lax.all_gather(first_gain, "shard", axis=0, tiled=True),
        lax.all_gather(first_offset, "shard", axis=0, tiled=True),
        lax.all_gather(in_weight, "shard", axis=0, tiled=True),
        lax.all_gather(query_bias, "shard", axis=0, tiled=True),
        lax.all_gather(value_bias, "shard", axis=0, tiled=True),
        lax.all_gather(out_weight, "shard", axis=0, tiled=True),
        lax.all_gather(out_bias, "shard", axis=0, tiled=True),
        lax.all_gather(second_gain, "shard", axis=0, tiled=True),
        lax.all_gather(second_offset, "shard", axis=0, tiled=True),
        lax.all_gather(up_weight, "shard", axis=0, tiled=True),
        lax.all_gather(up_bias, "shard", axis=0, tiled=True),
        lax.all_gather(down_weight, "shard", axis=0, tiled=True),
        lax.all_gather(down_bias, "shard", axis=0, tiled=True),
    )
    inputs = tokens.reshape(tok_dev, width).astype(floating)
    normed_in, unit_one, inverse_one = layer_norm(
        inputs, gain_one.astype(floating), offset_one.astype(floating)
    )
    normed_low = normed_in.astype(halfwidth)
    projected = jnp.dot(normed_low, weight_in, preferred_element_type=floating)
    query_low = (projected[:, :width] + bias_query.astype(floating)).astype(halfwidth)
    key_low = projected[:, width : 2 * width].astype(halfwidth)
    value_low = (projected[:, 2 * width :] + bias_value.astype(floating)).astype(halfwidth)
    query_ex, key_ex, value_ex = (
        lax.all_to_all(query_low, "seq", split_axis=1, concat_axis=0, tiled=True),
        lax.all_to_all(key_low, "seq", split_axis=1, concat_axis=0, tiled=True),
        lax.all_to_all(value_low, "seq", split_axis=1, concat_axis=0, tiled=True),
    )
    key_value = jnp.stack([key_ex, value_ex])
    collected = [key_value]
    for distance in range(1, SPAN):
        collected.append(passed_along(key_value, "shard", distance))
    joined = jnp.concatenate(collected, axis=1)
    key_heads = joined[0].reshape(SPAN * row_count, head_count, HEAD_DIM)
    value_heads = joined[1].reshape(SPAN * row_count, head_count, HEAD_DIM)
    block_rows = min(512, row_count)
    block_count = row_count // block_rows
    query_blocks = query_ex.reshape(block_count, block_rows, head_count, HEAD_DIM)
    starts = jnp.arange(block_count, dtype=jnp.int32) * block_rows
    attended, log_total = lax.map(
        lambda pieces: attend_block(
            pieces[0], pieces[1], key_heads, value_heads, row_count, position, factor
        ),
        (query_blocks, starts),
    )
    attended_low = attended.reshape(row_count, head_width).astype(halfwidth)
    attended_tok = lax.all_to_all(attended_low, "seq", split_axis=0, concat_axis=1, tiled=True)
    branch = jnp.dot(attended_tok, weight_out, preferred_element_type=floating) + bias_out.astype(
        floating
    )
    middle = inputs + branch
    normed_mid, unit_two, inverse_two = layer_norm(
        middle, gain_two.astype(floating), offset_two.astype(floating)
    )
    normed_mid_low = normed_mid.astype(halfwidth)
    pre_act = jnp.dot(normed_mid_low, weight_up, preferred_element_type=floating) + bias_up.astype(
        floating
    )
    activated, gelu_pull = jax.vjp(gelu_tanh, pre_act)
    activated_low = activated.astype(halfwidth)
    result = (
        middle
        + jnp.dot(activated_low, weight_down, preferred_element_type=floating)
        + bias_down.astype(floating)
    )
    gain_one, weight_in, weight_out, gain_two, weight_up, weight_down = (
        lax.all_gather(first_gain, "shard", axis=0, tiled=True),
        lax.all_gather(in_weight, "shard", axis=0, tiled=True),
        lax.all_gather(out_weight, "shard", axis=0, tiled=True),
        lax.all_gather(second_gain, "shard", axis=0, tiled=True),
        lax.all_gather(up_weight, "shard", axis=0, tiled=True),
        lax.all_gather(down_weight, "shard", axis=0, tiled=True),
    )
    upstream_low = cotangent.reshape(tok_dev, width)
    upstream = upstream_low.astype(floating)
    grad_down_bias = jnp.sum(upstream, axis=0)
    grad_down = jnp.einsum(
        "tf,td->fd", activated_low, upstream_low, preferred_element_type=floating
    )
    grad_act = jnp.einsum("td,fd->tf", upstream_low, weight_down, preferred_element_type=floating)
    grad_pre = gelu_pull(grad_act)[0].astype(halfwidth)
    grad_up_bias = jnp.sum(grad_pre.astype(floating), axis=0)
    grad_up = jnp.einsum("td,tf->df", normed_mid_low, grad_pre, preferred_element_type=floating)
    grad_mid_norm = jnp.einsum("tf,df->td", grad_pre, weight_up, preferred_element_type=floating)
    grad_gain_two = jnp.sum(grad_mid_norm * unit_two, axis=0)
    grad_offset_two = jnp.sum(grad_mid_norm, axis=0)
    grad_middle = upstream + norm_backward(
        grad_mid_norm, unit_two, inverse_two, gain_two.astype(floating)
    )
    grad_branch = grad_middle.astype(halfwidth)
    grad_out_bias = jnp.sum(grad_branch.astype(floating), axis=0)
    grad_out = jnp.einsum("td,te->de", attended_tok, grad_branch, preferred_element_type=floating)
    grad_attended = jnp.einsum(
        "te,de->td", grad_branch, weight_out, preferred_element_type=floating
    ).astype(halfwidth)
    grad_heads = lax.all_to_all(grad_attended, "seq", split_axis=1, concat_axis=0, tiled=True)
    grad_blocks = grad_heads.reshape(block_count, block_rows, head_count, HEAD_DIM)
    grad_query, grad_key, grad_value = lax.map(
        lambda pieces: attend_back(
            pieces[0],
            pieces[1],
            pieces[2],
            pieces[3],
            pieces[4],
            key_heads,
            value_heads,
            row_count,
            position,
            factor,
        ),
        (query_blocks, grad_blocks, attended, log_total, starts),
    )
    grad_query = grad_query.reshape(row_count, head_width)
    key_grads = jnp.stack([jnp.sum(grad_key, axis=0), jnp.sum(grad_value, axis=0)]).reshape(
        2, SPAN, row_count, head_width
    )
    owned = key_grads[:, 0]
    for distance in range(1, SPAN):
        owned = owned + passed_along(
            key_grads[:, distance].astype(jnp.bfloat16), "shard", -distance
        ).astype(jnp.float32)
    grad_q_tok, grad_k_tok, grad_v_tok = (
        lax.all_to_all(
            grad_query.astype(halfwidth), "seq", split_axis=0, concat_axis=1, tiled=True
        ),
        lax.all_to_all(owned[0].astype(halfwidth), "seq", split_axis=0, concat_axis=1, tiled=True),
        lax.all_to_all(owned[1].astype(halfwidth), "seq", split_axis=0, concat_axis=1, tiled=True),
    )
    grad_proj = jnp.concatenate([grad_q_tok, grad_k_tok, grad_v_tok], axis=1)
    grad_query_bias = jnp.sum(grad_q_tok.astype(floating), axis=0)
    grad_value_bias = jnp.sum(grad_v_tok.astype(floating), axis=0)
    grad_in = jnp.einsum("td,tf->df", normed_low, grad_proj, preferred_element_type=floating)
    grad_normed = jnp.einsum("tf,df->td", grad_proj, weight_in, preferred_element_type=floating)
    grad_gain_one = jnp.sum(grad_normed * unit_one, axis=0)
    grad_offset_one = jnp.sum(grad_normed, axis=0)
    grad_input = grad_middle + norm_backward(
        grad_normed, unit_one, inverse_one, gain_one.astype(floating)
    )
    slices = (
        lax.psum_scatter(grad_gain_one, "shard", scatter_dimension=0, tiled=True),
        lax.psum_scatter(grad_offset_one, "shard", scatter_dimension=0, tiled=True),
        lax.psum_scatter(grad_in, "shard", scatter_dimension=0, tiled=True),
        lax.psum_scatter(grad_query_bias, "shard", scatter_dimension=0, tiled=True),
        lax.psum_scatter(grad_value_bias, "shard", scatter_dimension=0, tiled=True),
        lax.psum_scatter(grad_out, "shard", scatter_dimension=0, tiled=True),
        lax.psum_scatter(grad_out_bias, "shard", scatter_dimension=0, tiled=True),
        lax.psum_scatter(grad_gain_two, "shard", scatter_dimension=0, tiled=True),
        lax.psum_scatter(grad_offset_two, "shard", scatter_dimension=0, tiled=True),
        lax.psum_scatter(grad_up, "shard", scatter_dimension=0, tiled=True),
        lax.psum_scatter(grad_up_bias, "shard", scatter_dimension=0, tiled=True),
        lax.psum_scatter(grad_down, "shard", scatter_dimension=0, tiled=True),
        lax.psum_scatter(grad_down_bias, "shard", scatter_dimension=0, tiled=True),
    )
    summed = (
        lax.psum(slices[0].astype(jnp.bfloat16), "seq").astype(jnp.float32),
        lax.psum(slices[1].astype(jnp.bfloat16), "seq").astype(jnp.float32),
        lax.psum(slices[2].astype(jnp.bfloat16), "seq").astype(jnp.float32),
        lax.psum(slices[3].astype(jnp.bfloat16), "seq").astype(jnp.float32),
        lax.psum(slices[4].astype(jnp.bfloat16), "seq").astype(jnp.float32),
        lax.psum(slices[5].astype(jnp.bfloat16), "seq").astype(jnp.float32),
        lax.psum(slices[6].astype(jnp.bfloat16), "seq").astype(jnp.float32),
        lax.psum(slices[7].astype(jnp.bfloat16), "seq").astype(jnp.float32),
        lax.psum(slices[8].astype(jnp.bfloat16), "seq").astype(jnp.float32),
        lax.psum(slices[9].astype(jnp.bfloat16), "seq").astype(jnp.float32),
        lax.psum(slices[10].astype(jnp.bfloat16), "seq").astype(jnp.float32),
        lax.psum(slices[11].astype(jnp.bfloat16), "seq").astype(jnp.float32),
        lax.psum(slices[12].astype(jnp.bfloat16), "seq").astype(jnp.float32),
    )
    return (
        result.astype(halfwidth).reshape(tokens.shape),
        grad_input.astype(halfwidth).reshape(tokens.shape),
        summed[0],
        summed[1],
        summed[2],
        summed[3],
        summed[4],
        summed[5],
        summed[6],
        summed[7],
        summed[8],
        summed[9],
        summed[10],
        summed[11],
        summed[12],
    )


def solution(mesh):
    return jax.shard_map(
        local,
        mesh=mesh,
        in_specs=(
            P("shard", "seq", None, None),
            P("shard", "seq", None, None),
            P("shard"),
            P("shard"),
            P("shard", None),
            P("shard"),
            P("shard"),
            P("shard", None),
            P("shard"),
            P("shard"),
            P("shard"),
            P("shard", None),
            P("shard"),
            P("shard", None),
            P("shard"),
        ),
        out_specs=(
            P("shard", "seq", None, None),
            P("shard", "seq", None, None),
            P("shard"),
            P("shard"),
            P("shard", None),
            P("shard"),
            P("shard"),
            P("shard", None),
            P("shard"),
            P("shard"),
            P("shard"),
            P("shard", None),
            P("shard"),
            P("shard", None),
            P("shard"),
        ),
        check_vma=False,
    )
```

profile of v0, /device:TPU:1, one launch (start us, length us, event | category | flops | bytes accessed | tf_op | source)
XLA Modules:
  0.0 1406.7 jit_solution(16225992610178779923)
XLA Ops:
  20.2 326.8 %all-reduce.25 = (bf16[768]{0:T(1024)(128)(2,1)S(1)}, bf16[768]{0:T(1024)(128)(2,1)S(1)}, bf16[768]{0:T(1024)(128)(2,1)S(1)}, bf16[768]{0:T(1024)(128)(2,1)S(1)}...) all-reduce(bf16[768]{0:T(1024)(128)(2,1)S(1)} %dynamic-update-slice, ...), channel_id=1, replica_groups=mesh['seq'=2,'shard'=64] {'shard'}, use_global_device_ids=true, to_apply=%add.1 | all-reduce | flops 9216 | bytes 36864
  350.3 4.9 reshape.297
  369.4 4.0 all-to-all-done.1
  376.1 8.4 collective-permute-start
  388.9 6.5 all-to-all-done.2
  412.5 7.5 reshape.301
  420.0 4.4 convolution_add_fusion
  424.4 5.9 convert_reduce_fusion
  436.5 4.1 all-to-all-start.4
  449.0 5.9 fusion.17
  471.6 9.1 collective-permute-start.3
  483.6 5.3 fusion.55
  496.1 4.8 collective-permute-done.4
  506.8 5.0 fusion.79
  520.4 4.2 fusion.52
  524.6 296.9 %fusion.80 = (f32[16,2304]{1,0:T(8,128)S(1)}, f32[16,768]{1,0:T(8,128)S(1)}, f32[16,3072]{1,0:T(8,128)S(1)}) fusion(f32[768,2304]{1,0:T(8,128)} %fusion.52, f32[768,768]{1,0:T(8,128)} %fusion.69, f32[768,3072]{1,0:T(8,128)} %fusion.79), kind=kCustom, calls=%all-reduce-scatter.3 | all-reduce-scatter fusion | flops 6291457 | bytes 19268096
  823.6 5.5 collective-permute-start.24
  832.2 4.6 collective-permute-start.26
  840.1 5.8 collective-permute-start.29
  847.9 12.3 collective-permute-start.30
  864.8 4.2 collective-permute-start.33
  870.3 4.1 fusion.26
  882.7 4.6 collective-permute-start.7
  890.6 6.4 collective-permute-start.10
  902.2 4.2 fusion.48
  935.2 5.5 collective-permute-start.42
  940.8 4.0 collective-permute-start.43
  945.0 315.8 %all-reduce.24 = (bf16[768]{0:T(1024)(128)(2,1)S(1)}, bf16[768]{0:T(1024)(128)(2,1)S(1)}, bf16[768]{0:T(1024)(128)(2,1)S(1)}, bf16[768]{0:T(1024)(128)(2,1)S(1)}...) all-reduce(f32[768]{0:T(1024)S(1)} %get-tuple-element.60, ...), channel_id=2, replica_groups=mesh['seq'=2,'shard'=64] {'shard'}, use_global_device_ids=true, to_apply=%region_12.13.clone | all-reduce | flops 9216 | bytes 55296
  1278.9 16.4 %concatenate.9 = bf16[268,2304]{1,0:T(8,128)(2,1)S(1)} concatenate(bf16[12,2304]{1,0:T(8,128)(2,1)} %copy-done.29, bf16[16,2304]{1,0:T(8,128)(2,1)} %collective-permute-done.20, bf16[16,2304]{1,0:T(8,128)(2,1)} %collective-permute-done.19, bf16[16,2304]{1,0:T(8,128)(2,1)} %copy-done.41, bf16[16,2304]{1,0:T(8,128)(2,1)} %copy-done.40, bf16[16,2304]{1,0:T(8,128)(2,1)} %copy-done.39, ...), dimensions={0} | concatenate | bytes 2543616
  1297.2 20.4 %collective-permute-start.50 = (bf16[16,3072]{1,0:T(8,128)(2,1)S(1)}, bf16[16,3072]{1,0:T(8,128)(2,1)}, u32[]{:S(2)}, u32[]{:S(2)}) collective-permute-start(bf16[16,3072]{1,0:T(8,128)(2,1)S(1)} %convert.108), channel_id=1, source_target_pairs={{0,13},{1,14},{2,15},{3,16},{4,17},{5,18},{6,19},{7,20},{8,21},{9,... | collective-permute-start | bytes 294920
  1327.7 38.5 %concatenate.11 = bf16[268,3072]{1,0:T(8,128)(2,1)} concatenate(bf16[12,3072]{1,0:T(8,128)(2,1)S(1)} %collective-permute-done.53, bf16[16,3072]{1,0:T(8,128)(2,1)} %collective-permute-done.52, bf16[16,3072]{1,0:T(8,128)(2,1)} %collective-permute-done.51, bf16[16,3072]{1,0:T(8,128)(2,1)} %collective-permute-done.50, bf16[16,3072]{1,0:T(8,128)(2,1)S(1)} %collective-permute-done.49, ...), dimensions={0} | concatenate | bytes 3391488
  1383.5 12.8 all-reduce.34.cloned.1.call-done
  (410 shorter events, 218.3 us)
Async XLA Ops:
  7.2 343.1 %all-gather.10.cloned.1.call-start = ((), (), s32[]{:S(2)}) async-start(), calls=%async_computation.11 | async-start | bytes 4792320 | tf_op jit(solution)/shard_map/all_gather | solution.py:144
  7.9 400.0 %all-gather.12.cloned.1.call-start = ((), (), s32[]{:S(2)}) async-start(), calls=%async_computation.12 | async-start | bytes 1597440 | tf_op jit(solution)/shard_map/all_gather | solution.py:147
  8.7 403.8 %all-gather.14.cloned.1.call-start = ((), (), s32[]{:S(2)}) async-start(), calls=%async_computation.13 | async-start | bytes 6389760 | tf_op jit(solution)/shard_map/all_gather | solution.py:151
  9.4 415.0 %all-gather.8.cloned.1.call-start = ((), (), s32[]{:S(2)}) async-start(), calls=%async_computation.9 | async-start | bytes 4792320 | tf_op jit(solution)/shard_map/all_gather | solution.py:153
  373.4 22.3 %collective-permute-start.2 = (bf16[2,256,384]{2,1,0:T(8,128)(2,1)S(1)}, bf16[2,256,384]{2,1,0:T(8,128)(2,1)S(1)}, u32[]{:S(2)}, u32[]{:S(2)}) collective-permute-start(bf16[2,256,384]{2,1,0:T(8,128)(2,1)S(1)} %pad_maximum_fusion.3), channel_id=1, source_target_pairs={{0,3},{1,4},{2,5},{3,6},{4,7},{5,8},{6,9},{7,10},{8,11},{9,12},{10... | collective-permute-start | bytes 1179656 | tf_op jit(solution)/shard_map/ppermute | solution.py:13
  374.7 20.9 %collective-permute-start.1 = (bf16[2,256,384]{2,1,0:T(8,128)(2,1)S(1)}, bf16[2,256,384]{2,1,0:T(8,128)(2,1)S(1)}, u32[]{:S(2)}, u32[]{:S(2)}) collective-permute-start(bf16[2,256,384]{2,1,0:T(8,128)(2,1)S(1)} %pad_maximum_fusion.3), channel_id=1, source_target_pairs={{0,2},{1,3},{2,4},{3,5},{4,6},{5,7},{6,8},{7,9},{8,10},{9,11},{10,... | collective-permute-start | bytes 1179656 | tf_op jit(solution)/shard_map/ppermute | solution.py:13
  376.1 19.6 %collective-permute-start = (bf16[2,256,384]{2,1,0:T(8,128)(2,1)S(1)}, bf16[2,256,384]{2,1,0:T(8,128)(2,1)S(1)}, u32[]{:S(2)}, u32[]{:S(2)}) collective-permute-start(bf16[2,256,384]{2,1,0:T(8,128)(2,1)S(1)} %pad_maximum_fusion.3), channel_id=1, source_target_pairs={{0,1},{1,2},{2,3},{3,4},{4,5},{5,6},{6,7},{7,8},{8,9},{9,10},{10,1... | collective-permute-start | bytes 1179656 | tf_op jit(solution)/shard_map/ppermute | solution.py:13
  440.6 927.1 %reduce-scatter.8.cloned.1.call-start = ((), (), s32[]{:S(2)}) async-start(), calls=%async_computation.10 | async-start | bytes 9584640 | tf_op jit(solution)/shard_map/reduce_scatter | solution.py:292
  471.6 24.4 %collective-permute-start.3 = (bf16[2,256,384]{2,1,0:T(8,128)(2,1)}, bf16[2,256,384]{2,1,0:T(8,128)(2,1)}, u32[]{:S(2)}, u32[]{:S(2)}) collective-permute-start(bf16[2,256,384]{2,1,0:T(8,128)(2,1)} %get-tuple-element.116), channel_id=1, source_target_pairs={{1,0},{2,1},{3,2},{4,3},{5,4},{6,5},{7,6},{8,7},{9,8},{10,9},{11,1... | collective-permute-start | bytes 1179656 | tf_op jit(solution)/shard_map/ppermute | solution.py:13
  482.0 18.8 %collective-permute-start.4 = (bf16[2,256,384]{2,1,0:T(8,128)(2,1)}, bf16[2,256,384]{2,1,0:T(8,128)(2,1)}, u32[]{:S(2)}, u32[]{:S(2)}) collective-permute-start(bf16[2,256,384]{2,1,0:T(8,128)(2,1)} %get-tuple-element.118), channel_id=1, source_target_pairs={{2,0},{3,1},{4,2},{5,3},{6,4},{7,5},{8,6},{9,7},{10,8},{11,9},{12,... | collective-permute-start | bytes 1179656 | tf_op jit(solution)/shard_map/ppermute | solution.py:13
  516.1 854.1 %all-reduce.32.cloned.1.call-start = ((), (), s32[]{:S(2)}) async-start(), calls=%async_computation.14 | async-start | bytes 205824 | tf_op jit(solution)/shard_map/psum | solution.py:296
  832.2 27.9 %collective-permute-start.26 = (bf16[16,768]{1,0:T(8,128)(2,1)S(1)}, bf16[16,768]{1,0:T(8,128)(2,1)S(1)}, u32[]{:S(2)}, u32[]{:S(2)}) collective-permute-start(bf16[16,768]{1,0:T(8,128)(2,1)S(1)} %convert.110), channel_id=1, source_target_pairs={{0,5},{1,6},{2,7},{3,8},{4,9},{5,10},{6,11},{7,12},{8,13},{9,14},{... | collective-permute-start | bytes 73736
  836.9 26.4 %collective-permute-start.27 = (bf16[16,768]{1,0:T(8,128)(2,1)S(1)}, bf16[16,768]{1,0:T(8,128)(2,1)S(1)}, u32[]{:S(2)}, u32[]{:S(2)}) collective-permute-start(bf16[16,768]{1,0:T(8,128)(2,1)S(1)} %convert.110), channel_id=1, source_target_pairs={{0,6},{1,7},{2,8},{3,9},{4,10},{5,11},{6,12},{7,13},{8,14},{9,15},... | collective-permute-start | bytes 73736
  838.2 26.6 %collective-permute-start.28 = (bf16[16,768]{1,0:T(8,128)(2,1)S(1)}, bf16[16,768]{1,0:T(8,128)(2,1)}, u32[]{:S(2)}, u32[]{:S(2)}) collective-permute-start(bf16[16,768]{1,0:T(8,128)(2,1)S(1)} %convert.110), channel_id=1, source_target_pairs={{0,7},{1,8},{2,9},{3,10},{4,11},{5,12},{6,13},{7,14},{8,15},{9,16}... | collective-permute-start | bytes 73736
  840.1 28.9 %collective-permute-start.29 = (bf16[16,768]{1,0:T(8,128)(2,1)S(1)}, bf16[16,768]{1,0:T(8,128)(2,1)}, u32[]{:S(2)}, u32[]{:S(2)}) collective-permute-start(bf16[16,768]{1,0:T(8,128)(2,1)S(1)} %convert.110), channel_id=1, source_target_pairs={{0,8},{1,9},{2,10},{3,11},{4,12},{5,13},{6,14},{7,15},{8,16},{9,17... | collective-permute-start | bytes 73736
  847.9 26.6 %collective-permute-start.30 = (bf16[16,768]{1,0:T(8,128)(2,1)S(1)}, bf16[16,768]{1,0:T(8,128)(2,1)S(1)}, u32[]{:S(2)}, u32[]{:S(2)}) collective-permute-start(bf16[16,768]{1,0:T(8,128)(2,1)S(1)} %convert.110), channel_id=1, source_target_pairs={{0,9},{1,10},{2,11},{3,12},{4,13},{5,14},{6,15},{7,16},{8,17},{9,1... | collective-permute-start | bytes 73736
  887.7 18.8 %collective-permute-start.8 = (bf16[16,2304]{1,0:T(8,128)(2,1)S(1)}, bf16[16,2304]{1,0:T(8,128)(2,1)S(1)}, u32[]{:S(2)}, u32[]{:S(2)}) collective-permute-start(bf16[16,2304]{1,0:T(8,128)(2,1)S(1)} %convert.109), channel_id=1, source_target_pairs={{0,3},{1,4},{2,5},{3,6},{4,7},{5,8},{6,9},{7,10},{8,11},{9,12},{10... | collective-permute-start | bytes 221192
  889.1 19.0 %collective-permute-start.9 = (bf16[16,2304]{1,0:T(8,128)(2,1)S(1)}, bf16[16,2304]{1,0:T(8,128)(2,1)S(1)}, u32[]{:S(2)}, u32[]{:S(2)}) collective-permute-start(bf16[16,2304]{1,0:T(8,128)(2,1)S(1)} %convert.109), channel_id=1, source_target_pairs={{0,4},{1,5},{2,6},{3,7},{4,8},{5,9},{6,10},{7,11},{8,12},{9,13},{1... | collective-permute-start | bytes 221192
  890.6 21.3 %collective-permute-start.10 = (bf16[16,2304]{1,0:T(8,128)(2,1)S(1)}, bf16[16,2304]{1,0:T(8,128)(2,1)S(1)}, u32[]{:S(2)}, u32[]{:S(2)}) collective-permute-start(bf16[16,2304]{1,0:T(8,128)(2,1)S(1)} %convert.109), channel_id=1, source_target_pairs={{0,5},{1,6},{2,7},{3,8},{4,9},{5,10},{6,11},{7,12},{8,13},{9,14},{... | collective-permute-start | bytes 221192
  928.3 341.6 %collective-permute-start.39 = (bf16[16,3072]{1,0:T(8,128)(2,1)S(1)}, bf16[16,3072]{1,0:T(8,128)(2,1)S(1)}, u32[]{:S(2)}, u32[]{:S(2)}) collective-permute-start(bf16[16,3072]{1,0:T(8,128)(2,1)S(1)} %convert.108), channel_id=1, source_target_pairs={{0,2},{1,3},{2,4},{3,5},{4,6},{5,7},{6,8},{7,9},{8,10},{9,11},{10,... | collective-permute-start | bytes 294920
  931.7 339.5 %collective-permute-start.40 = (bf16[16,3072]{1,0:T(8,128)(2,1)S(1)}, bf16[16,3072]{1,0:T(8,128)(2,1)S(1)}, u32[]{:S(2)}, u32[]{:S(2)}) collective-permute-start(bf16[16,3072]{1,0:T(8,128)(2,1)S(1)} %convert.108), channel_id=1, source_target_pairs={{0,3},{1,4},{2,5},{3,6},{4,7},{5,8},{6,9},{7,10},{8,11},{9,12},{10... | collective-permute-start | bytes 294920
  933.0 339.5 %collective-permute-start.41 = (bf16[16,3072]{1,0:T(8,128)(2,1)S(1)}, bf16[16,3072]{1,0:T(8,128)(2,1)S(1)}, u32[]{:S(2)}, u32[]{:S(2)}) collective-permute-start(bf16[16,3072]{1,0:T(8,128)(2,1)S(1)} %convert.108), channel_id=1, source_target_pairs={{0,4},{1,5},{2,6},{3,7},{4,8},{5,9},{6,10},{7,11},{8,12},{9,13},{1... | collective-permute-start | bytes 294920
  935.2 339.2 %collective-permute-start.42 = (bf16[16,3072]{1,0:T(8,128)(2,1)S(1)}, bf16[16,3072]{1,0:T(8,128)(2,1)S(1)}, u32[]{:S(2)}, u32[]{:S(2)}) collective-permute-start(bf16[16,3072]{1,0:T(8,128)(2,1)S(1)} %convert.108), channel_id=1, source_target_pairs={{0,5},{1,6},{2,7},{3,8},{4,9},{5,10},{6,11},{7,12},{8,13},{9,14},{... | collective-permute-start | bytes 294920
  940.8 335.6 %collective-permute-start.43 = (bf16[16,3072]{1,0:T(8,128)(2,1)S(1)}, bf16[16,3072]{1,0:T(8,128)(2,1)S(1)}, u32[]{:S(2)}, u32[]{:S(2)}) collective-permute-start(bf16[16,3072]{1,0:T(8,128)(2,1)S(1)} %convert.108), channel_id=1, source_target_pairs={{0,6},{1,7},{2,8},{3,9},{4,10},{5,11},{6,12},{7,13},{8,14},{9,15},... | collective-permute-start | bytes 294920
  1269.9 25.5 %collective-permute-start.44 = (bf16[16,3072]{1,0:T(8,128)(2,1)S(1)}, bf16[16,3072]{1,0:T(8,128)(2,1)S(1)}, u32[]{:S(2)}, u32[]{:S(2)}) collective-permute-start(bf16[16,3072]{1,0:T(8,128)(2,1)S(1)} %convert.108), channel_id=1, source_target_pairs={{0,7},{1,8},{2,9},{3,10},{4,11},{5,12},{6,13},{7,14},{8,15},{9,16}... | collective-permute-start | bytes 294920
  1271.2 26.0 %collective-permute-start.45 = (bf16[16,3072]{1,0:T(8,128)(2,1)S(1)}, bf16[16,3072]{1,0:T(8,128)(2,1)S(1)}, u32[]{:S(2)}, u32[]{:S(2)}) collective-permute-start(bf16[16,3072]{1,0:T(8,128)(2,1)S(1)} %convert.108), channel_id=1, source_target_pairs={{0,8},{1,9},{2,10},{3,11},{4,12},{5,13},{6,14},{7,15},{8,16},{9,17... | collective-permute-start | bytes 294920
  1272.5 45.1 %collective-permute-start.46 = (bf16[16,3072]{1,0:T(8,128)(2,1)S(1)}, bf16[16,3072]{1,0:T(8,128)(2,1)}, u32[]{:S(2)}, u32[]{:S(2)}) collective-permute-start(bf16[16,3072]{1,0:T(8,128)(2,1)S(1)} %convert.108), channel_id=1, source_target_pairs={{0,9},{1,10},{2,11},{3,12},{4,13},{5,14},{6,15},{7,16},{8,17},{9,1... | collective-permute-start | bytes 294920
  1274.4 46.9 %collective-permute-start.47 = (bf16[16,3072]{1,0:T(8,128)(2,1)S(1)}, bf16[16,3072]{1,0:T(8,128)(2,1)}, u32[]{:S(2)}, u32[]{:S(2)}) collective-permute-start(bf16[16,3072]{1,0:T(8,128)(2,1)S(1)} %convert.108), channel_id=1, source_target_pairs={{0,10},{1,11},{2,12},{3,13},{4,14},{5,15},{6,16},{7,17},{8,18},{9,... | collective-permute-start | bytes 294920
  1276.4 46.9 %collective-permute-start.48 = (bf16[16,3072]{1,0:T(8,128)(2,1)S(1)}, bf16[16,3072]{1,0:T(8,128)(2,1)}, u32[]{:S(2)}, u32[]{:S(2)}) collective-permute-start(bf16[16,3072]{1,0:T(8,128)(2,1)S(1)} %convert.108), channel_id=1, source_target_pairs={{0,11},{1,12},{2,13},{3,14},{4,15},{5,16},{6,17},{7,18},{8,19},{9,... | collective-permute-start | bytes 294920
  1295.3 31.5 %collective-permute-start.49 = (bf16[16,3072]{1,0:T(8,128)(2,1)S(1)}, bf16[16,3072]{1,0:T(8,128)(2,1)S(1)}, u32[]{:S(2)}, u32[]{:S(2)}) collective-permute-start(bf16[16,3072]{1,0:T(8,128)(2,1)S(1)} %convert.108), channel_id=1, source_target_pairs={{0,12},{1,13},{2,14},{3,15},{4,16},{5,17},{6,18},{7,19},{8,20},{9,... | collective-permute-start | bytes 294920
  1297.2 29.6 %collective-permute-start.50 = (bf16[16,3072]{1,0:T(8,128)(2,1)S(1)}, bf16[16,3072]{1,0:T(8,128)(2,1)}, u32[]{:S(2)}, u32[]{:S(2)}) collective-permute-start(bf16[16,3072]{1,0:T(8,128)(2,1)S(1)} %convert.108), channel_id=1, source_target_pairs={{0,13},{1,14},{2,15},{3,16},{4,17},{5,18},{6,19},{7,20},{8,21},{9,... | collective-permute-start | bytes 294920
  1326.8 69.5 %all-reduce.34.cloned.1.call-start = ((), (), s32[]{:S(2)}) async-start(), calls=%async_computation.15 | async-start | bytes 344064 | tf_op jit(solution)/shard_map/psum | solution.py:305
  (115 other events, 8118.9 us)
Sparse Core Ops, SparseCore 0:
  11.1 76.6 all-gather.9
  90.8 65.4 all-gather.11
  159.4 73.6 all-gather.13
  235.9 71.9 all-gather.7
  489.0 195.6 reduce-scatter.7
  1326.8 25.6 all-reduce.31
  1369.4 26.8 all-reduce.33
where the time goes:
time: 1420 us; the launch traced here: 1410 us
  blocking collectives  939 us (66%)
  starting transfers between devices  201 us (14%)
  local copies, waits for them, and re-layouts  118 us (8%)
  matrix products  56.4 us (4%)
  waiting for transfers between devices  40.4 us (3%)
  other arithmetic  30.9 us (2%)
  between operations  19.9 us (1%)
    unnamed x3, blocking collectives  939 us
    unnamed x48, starting transfers between devices  150 us
    unnamed x193, local copies, waits for them, and re-layouts  93.8 us
  transfers between devices with their start and end apart: 69, of which 9 were waited for; matrix products, arithmetic and copies ran while one was open for 32% of the time, Pallas kernels for 0%

commit v1 on v0

v1 whole, which is shorter than its diff:
```python
import jax
import jax.numpy as jnp
from jax import lax
from jax.sharding import Mesh, PartitionSpec as P

HEAD_DIM = 64
HEADS = 12
WIDTH = 768
HIDDEN = 3072
TOK = 128
RING = ("xl", "xh")
CHIPS = ("xl", "z", "y", "xh")
SHARD = ("z", "y", "xh", "c")
SWAP = [(0, 1), (1, 0)]
F32 = jnp.float32
BF16 = jnp.bfloat16


def ring_index(place):
    return (place % 2) * 2 + place // 2


def ring_shift(value, steps):
    pairs = [(ring_index(i), ring_index((i + steps) % 4)) for i in range(4)]
    return lax.ppermute(value, RING, pairs)


def mirror(value):
    pairs = [(ring_index(i), ring_index(3 - i)) for i in range(4)]
    return lax.ppermute(value, RING, pairs)


def core_swap(value):
    return lax.ppermute(value, "c", SWAP)


def ordered(flag, own, other, axis):
    return jnp.where(
        flag == 0,
        jnp.concatenate([own, other], axis=axis),
        jnp.concatenate([other, own], axis=axis),
    )


def half_of(value, which, axis):
    size = value.shape[axis] // 2
    return lax.dynamic_slice_in_dim(value, which * size, size, axis)


def gelu_tanh(inputs):
    return (
        0.5
        * inputs
        * (1.0 + jnp.tanh(0.7978845608028654 * (inputs + 0.044715 * inputs * inputs * inputs)))
    )


def normed_of(values):
    average = jnp.mean(values, axis=-1, keepdims=True)
    centered = values - average
    inverse = lax.rsqrt(jnp.mean(centered * centered, axis=-1, keepdims=True) + 1e-05)
    return centered * inverse, inverse


def norm_backward(upstream, normed, inverse, norm_gain):
    scaled = upstream * norm_gain
    return inverse * (
        scaled
        - jnp.mean(scaled, axis=-1, keepdims=True)
        - normed * jnp.mean(scaled * normed, axis=-1, keepdims=True)
    )


def gather_tokens(own):
    ring = jnp.stack([own] + [ring_shift(own, steps) for steps in (1, 2, 3)])
    return jnp.concatenate([ring, core_swap(ring)])


def gather_weights(core, xh, pieces):
    in_weight, out_weight, up_weight, down_weight, vectors, up_bias = pieces
    wide = jnp.concatenate([in_weight, out_weight, up_weight], axis=1)
    small = jnp.concatenate(
        [jnp.stack(vectors, axis=1), up_bias.reshape(12, 4), jnp.zeros((12, 116), BF16)], axis=1
    )
    own = jnp.concatenate([half_of(wide, core, 1), small], axis=1)
    far = jnp.concatenate([half_of(wide, 1 - core, 1), small], axis=1)
    rows = ordered(core, own, core_swap(far), 0)
    rows = ordered(xh, rows, mirror(rows), 0)
    down = ordered(core, half_of(down_weight, core, 1), core_swap(half_of(down_weight, 1 - core, 1)), 0)
    down = ordered(xh, down, mirror(down), 0)
    packed = jnp.concatenate([rows] + [down[48 * k : 48 * k + 48] for k in range(4)], axis=1)
    full = lax.all_gather(packed, ("z", "y"), axis=0, tiled=True)
    wide_own = full[:, :3072]
    small = full[:, 3072:3084].astype(F32)
    down_own = full[:, 3200:]
    wide_other = core_swap(wide_own)
    down_other = core_swap(down_own)
    in_out = jnp.where(core == 0, wide_own, wide_other)
    up = jnp.where(core == 0, wide_other, wide_own)

    def rows_of(value):
        return value.reshape(16, 48, 4, 384).transpose(0, 2, 1, 3).reshape(HIDDEN, 384)

    down = ordered(core, rows_of(down_own), rows_of(down_other), 1)
    return in_out, up, down, small


def pair_halves(grad, core, axis):
    low = grad.astype(BF16)
    mine = half_of(grad, core, axis)
    return mine + core_swap(half_of(low, 1 - core, axis)).astype(F32)


def spread(blocks):
    got = lax.all_to_all(blocks.astype(BF16), CHIPS, 0, 0, tiled=True)
    return jnp.sum(got.astype(F32), axis=0)


def wide_blocks(grad):
    return grad.reshape(32, 24, 2, 2, 384).transpose(2, 0, 3, 1, 4).reshape(64, 48, 384)


def local(
    tokens,
    cotangent,
    first_gain,
    first_offset,
    in_weight,
    query_bias,
    value_bias,
    out_weight,
    out_bias,
    second_gain,
    second_offset,
    up_weight,
    up_bias,
    down_weight,
    down_bias,
):
    core = lax.axis_index("c")
    xh = lax.axis_index("xh")
    xl = lax.axis_index("xl")
    place = 2 * xh + xl
    own_tokens = tokens.reshape(TOK, WIDTH)
    group = gather_tokens(own_tokens).astype(F32).reshape(8 * TOK, WIDTH)
    vectors = (
        first_gain,
        first_offset,
        query_bias,
        value_bias,
        out_bias,
        second_gain,
        second_offset,
        down_bias,
    )
    in_out, weight_up, weight_down, small = gather_weights(
        core, xh, (in_weight, out_weight, up_weight, down_weight, vectors, up_bias)
    )
    gain_one, offset_one, bias_query, bias_value, bias_out, gain_two, offset_two, bias_down = (
        small[:, k] for k in range(8)
    )
    bias_up = small[:, 8:12].reshape(HIDDEN)
    weight_in = in_out[:, : 3 * WIDTH]
    weight_out = in_out[:, 3 * WIDTH :]

    blocks = []
    for other in (0, 1):
        for steps in range(4):
            there = (place + 4 - steps) % 4
            blocks.append(((there // 2) * 2 + (core + other) % 2) * 2 + there % 2)
    starts = jnp.stack(blocks) * TOK
    key_pos = (starts[:, None] + jnp.arange(TOK)[None]).reshape(-1)
    query_pos = starts[0] + jnp.arange(TOK)
    visible = key_pos[None, :] <= query_pos[:, None]

    unit_one, inverse_one = normed_of(group)
    normed_one = (unit_one * gain_one + offset_one).astype(BF16)
    own_normed = normed_one[:TOK]
    query = (
        jnp.dot(own_normed, weight_in[:, :WIDTH], preferred_element_type=F32) + bias_query
    ).astype(BF16)
    key_value = jnp.dot(normed_one, weight_in[:, WIDTH:], preferred_element_type=F32)
    key = key_value[:, :WIDTH].astype(BF16)
    value = (key_value[:, WIDTH:] + bias_value).astype(BF16)
    query_h = query.reshape(TOK, HEADS, HEAD_DIM)
    key_h = key.reshape(8 * TOK, HEADS, HEAD_DIM)
    value_h = value.reshape(8 * TOK, HEADS, HEAD_DIM)
    scores = jnp.einsum("qhd,khd->hqk", query_h, key_h, preferred_element_type=F32) * 0.125
    scores = jnp.where(visible[None], scores, -1e30)
    highest = jnp.max(scores, axis=-1, keepdims=True)
    exponent = jnp.exp(scores - highest)
    probs = exponent / jnp.sum(exponent, axis=-1, keepdims=True)
    probs_low = probs.astype(BF16)
    attended = jnp.einsum("hqk,khd->qhd", probs_low, value_h, preferred_element_type=F32)
    attended = attended.reshape(TOK, WIDTH).astype(BF16)
    own_float = own_tokens.astype(F32)
    middle = own_float + jnp.dot(attended, weight_out, preferred_element_type=F32) + bias_out
    unit_two, inverse_two = normed_of(middle)
    normed_two = (unit_two * gain_two + offset_two).astype(BF16)
    pre_act = jnp.dot(normed_two, weight_up, preferred_element_type=F32) + bias_up
    activated, gelu_pull = jax.vjp(gelu_tanh, pre_act)
    activated = activated.astype(BF16)
    result = middle + jnp.dot(activated, weight_down, preferred_element_type=F32) + bias_down

    upstream_low = cotangent.reshape(TOK, WIDTH)
    upstream = upstream_low.astype(F32)
    grad_down_bias = jnp.sum(upstream, axis=0)
    grad_down = jnp.einsum("tf,td->fd", activated, upstream_low, preferred_element_type=F32)
    grad_act = jnp.einsum("td,fd->tf", upstream_low, weight_down, preferred_element_type=F32)
    grad_pre_float = gelu_pull(grad_act)[0]
    grad_pre = grad_pre_float.astype(BF16)
    grad_up_bias = jnp.sum(grad_pre.astype(F32), axis=0)
    grad_up = jnp.einsum("td,tf->df", normed_two, grad_pre, preferred_element_type=F32)
    down_half = pair_halves(grad_down, core, 1)
    up_half = pair_halves(grad_up, core, 1)
    first_blocks = jnp.concatenate(
        [
            wide_blocks(up_half),
            down_half.reshape(32, 2, 2, 24, 384).transpose(2, 0, 1, 3, 4).reshape(64, 48, 384),
        ],
        axis=1,
    )
    first_sum = spread(first_blocks)

    grad_mid_norm = jnp.einsum("tf,df->td", grad_pre, weight_up, preferred_element_type=F32)
    grad_gain_two = jnp.sum(grad_mid_norm * unit_two, axis=0)
    grad_offset_two = jnp.sum(grad_mid_norm, axis=0)
    grad_middle = upstream + norm_backward(grad_mid_norm, unit_two, inverse_two, gain_two)
    grad_branch = grad_middle.astype(BF16)
    grad_out_bias = jnp.sum(grad_branch.astype(F32), axis=0)
    grad_out = jnp.einsum("td,te->de", attended, grad_branch, preferred_element_type=F32)
    grad_attended = jnp.einsum("te,de->td", grad_branch, weight_out, preferred_element_type=F32)
    grad_attended = grad_attended.astype(BF16).reshape(TOK, HEADS, HEAD_DIM)

    grad_probs = jnp.einsum("qhd,khd->hqk", grad_attended, value_h, preferred_element_type=F32)
    inner = jnp.sum(probs * grad_probs, axis=-1, keepdims=True)
    grad_scores = (probs * (grad_probs - inner)).astype(BF16)
    grad_query = (
        jnp.einsum("hqk,khd->qhd", grad_scores, key_h, preferred_element_type=F32) * 0.125
    )
    grad_query = grad_query.reshape(TOK, WIDTH).astype(BF16)
    grad_key = jnp.einsum("hqk,qhd->khd", grad_scores, query_h, preferred_element_type=F32) * 0.125
    grad_value = jnp.einsum("hqk,qhd->khd", probs_low, grad_attended, preferred_element_type=F32)
    grad_value = grad_value.reshape(8 * TOK, WIDTH)
    grad_kv = jnp.concatenate([grad_key.reshape(8 * TOK, WIDTH), grad_value], axis=1).astype(BF16)
    grad_query_bias = jnp.sum(grad_query.astype(F32), axis=0)
    grad_value_bias = jnp.sum(grad_value, axis=0)

    partial = jnp.einsum("tf,df->td", grad_kv, weight_in[:, WIDTH:], preferred_element_type=F32)
    partial = partial.reshape(8, TOK, WIDTH)
    ring = partial[:4] + core_swap(partial[4:].astype(BF16)).astype(F32)
    grad_normed = ring[0] + jnp.einsum(
        "tf,df->td", grad_query, weight_in[:, :WIDTH], preferred_element_type=F32
    )
    for steps in (1, 2, 3):
        grad_normed = grad_normed + ring_shift(ring[steps].astype(BF16), -steps).astype(F32)
    own_unit = unit_one[:TOK]
    grad_gain_one = jnp.sum(grad_normed * own_unit, axis=0)
    grad_offset_one = jnp.sum(grad_normed, axis=0)
    grad_input = grad_middle + norm_backward(grad_normed, own_unit, inverse_one[:TOK], gain_one)

    grad_in_q = jnp.einsum("td,tf->df", own_normed, grad_query, preferred_element_type=F32)
    grad_in_kv = jnp.einsum("td,tf->df", normed_one, grad_kv, preferred_element_type=F32)
    in_half = pair_halves(jnp.concatenate([grad_in_q, grad_in_kv, grad_out], axis=1), core, 1)
    second_sum = spread(wide_blocks(in_half))

    small_grads = jnp.stack(
        [
            grad_gain_one,
            grad_offset_one,
            grad_query_bias,
            grad_value_bias,
            grad_out_bias,
            grad_gain_two,
            grad_offset_two,
            grad_down_bias,
        ],
        axis=1,
    )
    small_grads = jnp.concatenate([small_grads, grad_up_bias.reshape(WIDTH, 4)], axis=1)
    small_grads = jnp.pad(small_grads.reshape(32, 2, 144), ((0, 0), (0, 6), (0, 112)))
    small_got = lax.all_to_all(jnp.concatenate([small_grads, small_grads]), CHIPS, 0, 0, tiled=True)
    small_sum = jnp.sum(small_got, axis=0)
    small_sum = small_sum + core_swap(small_sum)
    small_own = lax.dynamic_slice_in_dim(small_sum, core, 1, 0)[0, :144].reshape(12, 12)

    everything = jnp.concatenate([first_sum, second_sum])
    wide = jnp.concatenate([first_sum[:48], second_sum]).reshape(4, 2, 12, 384)
    down = first_sum[48:].reshape(2, 24, 384)
    wide_keep = half_of(wide, core, 1).reshape(48, 384)
    wide_send = half_of(wide, 1 - core, 1).reshape(48, 384)
    down_keep = half_of(down, core, 0).reshape(24, 384)
    down_send = half_of(down, 1 - core, 0).reshape(24, 384)
    keep = jnp.concatenate([wide_keep, down_keep]).astype(BF16)
    send = jnp.concatenate([wide_send, down_send]).astype(BF16)
    both = ordered(core, keep[None], core_swap(send)[None], 0)
    quad = ordered(xl, both[None], lax.ppermute(both[None], "xl", SWAP), 0).astype(F32)
    wide_own = quad[:, :, :48].reshape(2, 2, 2, 2, 12, 384)
    wide_own = wide_own.transpose(2, 4, 1, 0, 3, 5).reshape(2, 12, 3072)
    down_own = quad[:, :, 48:].transpose(0, 2, 1, 3).reshape(48, WIDTH)
    return (
        result.astype(BF16).reshape(tokens.shape),
        grad_input.astype(BF16).reshape(tokens.shape),
        small_own[:, 0],
        small_own[:, 1],
        wide_own[1][:, : 3 * WIDTH],
        small_own[:, 2],
        small_own[:, 3],
        wide_own[1][:, 3 * WIDTH :],
        small_own[:, 4],
        small_own[:, 5],
        small_own[:, 6],
        wide_own[0],
        small_own[:, 8:].reshape(48),
        down_own,
        small_own[:, 7],
    )


def solution(mesh):
    fine = Mesh(mesh.devices.reshape(2, 4, 4, 2, 2), ("xl", "z", "y", "xh", "c"))
    tok = P(SHARD, "xl", None, None)
    vec = P(SHARD)
    mat = P(SHARD, None)
    return jax.shard_map(
        local,
        mesh=fine,
        in_specs=(tok, tok, vec, vec, mat, vec, vec, mat, vec, vec, vec, mat, vec, mat, vec),
        out_specs=(tok, tok, vec, vec, mat, vec, vec, mat, vec, vec, vec, mat, vec, mat, vec),
        check_vma=False,
    )
```

time: 1420 us -> 429 us (0.30)
  blocking collectives: 939 us -> 0 us
  starting transfers between devices: 201 us -> 51.1 us
  waiting for transfers between devices: 40.4 us -> 142 us
  other arithmetic: 30.9 us -> 55.1 us
  local copies, waits for them, and re-layouts: 118 us -> 98.7 us
    unnamed x3 -> x0, blocking collectives: 939 us -> none
    unnamed x48 -> x0, starting transfers between devices: 150 us -> none
    unnamed x193 -> x92, local copies, waits for them, and re-layouts: 93.8 us -> 7.61 us
    all_gather x4 -> x1, waiting for transfers between devices: 0.05 us -> 68.3 us  [gather_weights(): full = lax.all_gather(packed, ('z', 'y'), axis=0, tiled=True)]
    all_to_all x8 -> x3, waiting for transfers between devices: 19.2 us -> 49.6 us  [the longest x2 49.6 us: spread(): got = lax.all_to_all(blocks.astype(BF16), CHIPS, 0, 0, tiled=True)]
    reshape x0 -> x11, local copies, waits for them, and re-layouts: none -> 24.1 us  [the longest x2 9.33 us: rows_of(): value.reshape(16, 48, 4, 384).transpose(0, 2, 1, 3).reshape(HIDDEN, 384)]
    ppermute x6 -> x20, waiting for transfers between devices: 4.78 us -> 23.6 us  [the longest x6 14.4 us: ring_shift(): return lax.ppermute(value, RING, pairs)]
    slice x5 -> x19, local copies, waits for them, and re-layouts: 0.8 us -> 17 us  [the longest x1 4.85 us: gather_weights(): wide_own = full[:, :3072]]
  transfers between devices with their start and end apart: 69 -> 24, of which waited for: 9 -> 12; matrix products, arithmetic and copies ran while one was open for 32% -> 28% of each run, Pallas kernels for 0% -> 0%
where the time goes in v1:
time: 429 us; the launch traced here: 423 us
  waiting for transfers between devices  142 us (33%)
  local copies, waits for them, and re-layouts  98.7 us (23%)
  matrix products  61.5 us (14%)
  other arithmetic  55.1 us (13%)
  starting transfers between devices  51.1 us (12%)
  between operations  15.2 us (4%)
    all_gather x1, waiting for transfers between devices, gather_weights(): full = lax.all_gather(packed, ('z', 'y'), axis=0, tiled=True)  68.3 us
    all_to_all x2, waiting for transfers between devices, spread(): got = lax.all_to_all(blocks.astype(BF16), CHIPS, 0, 0, tiled=True)  49.6 us
    all_to_all x2, starting transfers between devices, spread(): got = lax.all_to_all(blocks.astype(BF16), CHIPS, 0, 0, tiled=True)  16.5 us
    ppermute x11, starting transfers between devices, core_swap(): return lax.ppermute(value, 'c', SWAP)  14.5 us
    ppermute x6, waiting for transfers between devices, ring_shift(): return lax.ppermute(value, RING, pairs)  14.4 us
    another operation x3, other arithmetic  10.7 us
    another operation x8, local copies, waits for them, and re-layouts, local(): jnp.stack([grad_gain_one, grad_offset_one, grad_query_bias, grad_value_bi...  9.77 us
    reshape x2, local copies, waits for them, and re-layouts, rows_of(): value.reshape(16, 48, 4, 384).transpose(0, 2, 1, 3).reshape(HIDDEN, 384)  9.33 us
  transfers between devices with their start and end apart: 24, of which 12 were waited for; matrix products, arithmetic and copies ran while one was open for 28% of the time, Pallas kernels for 0%

profile of v1, /device:TPU:1, one launch (start us, length us, event | category | flops | bytes accessed | tf_op | source)
XLA Modules:
  0.0 423.2 jit_solution(1255189606169937229)
XLA Ops:
  23.7 4.2 %collective-permute-done.5 = bf16[24,3200]{1,0:T(8,128)(2,1)S(1)} collective-permute-done((bf16[24,3200]{1,0:T(8,128)(2,1)S(1)}, bf16[24,3200]{1,0:T(8,128)(2,1)S(1)}, u32[]{:S(2)}, u32[]{:S(2)}) %collective-permute-start.5) | collective-permute-done | bytes 153632 | tf_op jit(solution)/shard_map/ppermute | solution.py:30
  28.9 68.3 %all-gather.2.cloned.1.call-done = bf16[768,4736]{1,0:T(8,128)(2,1)} async-done(((bf16[48,4736]{1,0:T(8,128)(2,1)}), bf16[768,4736]{1,0:T(8,128)(2,1)}) %all-gather.2.cloned.1.call-update) | async-done | bytes 7274512 | tf_op jit(solution)/shard_map/all_gather | solution.py:92
  97.2 4.9 %slice.222 = bf16[768,3072]{1,0:T(8,128)(2,1)} slice(bf16[768,4736]{1,0:T(8,128)(2,1)} %all-gather.2.cloned.1.call-done), slice={[0:768], [0:3072]} | slice | bytes 9437184 | tf_op jit(solution)/shard_map/slice | solution.py:93
  110.8 4.5 %collective-permute-done = bf16[128,768]{1,0:T(8,128)(2,1)S(1)} collective-permute-done((bf16[128,768]{1,0:T(8,128)(2,1)S(1)}, bf16[128,768]{1,0:T(8,128)(2,1)S(1)}, u32[]{:S(2)}, u32[]{:S(2)}) %collective-permute-start) | collective-permute-done | bytes 196640 | tf_op jit(solution)/shard_map/ppermute | solution.py:25
  122.8 5.2 %reshape.466 = bf16[16,48,4,384]{3,2,1,0:T(4,128)(2,1)} reshape(bf16[768,1536]{1,0:T(8,128)(2,1)} %slice.235) | data formatting | bytes 4718592 | tf_op jit(solution)/shard_map/reshape | solution.py:102
  137.7 4.1 reshape.468
  143.8 4.4 %broadcast_select_fusion.1 = bf16[768,3072]{1,0:T(8,128)(2,1)S(1)} fusion(bf16[768,3072]{1,0:T(8,128)(2,1)} %collective-permute-done.8, pred[]{:T(512)S(6)} %eq.41, bf16[768,4736]{1,0:T(8,128)(2,1)} %all-gather.2.cloned.1.call-done), kind=kLoop, calls=%fused_computation.18 | loop fusion | flops 2359296 | bytes 14155777 | tf_op jit(solution)/shard_map/jit(_where)/select_n | solution.py:98
  148.1 4.6 %fusion.9 = f32[1024,1536]{1,0:T(8,128)} fusion(bf16[1024,768]{1,0:T(8,128)(2,1)S(1)} %copy-done.10, bf16[768,3072]{1,0:T(8,128)(2,1)S(1)} %broadcast_select_fusion.1), kind=kOutput, calls=%fused_computation.42 | convolution fusion | flops 2415919104 | bytes 10223616 | tf_op jit(solution)/shard_map/dot_general | solution.py:182
  159.4 3.7 copy.220
  163.2 5.1 %fusion.73 = (f32[12,128]{1,0:T(8,128)S(1)}, f32[12,128,1024]{2,1,0:T(8,128)}) fusion(pred[128,1024]{1,0:T(8,128)(4,1)S(1)} %copy-done.21, bf16[128,12,64]{0,2,1:T(8,128)(2,1)S(1)} %bitcast.176, bf16[1024,12,64]{0,2,1:T(8,128)(2,1)S(1)} %bitcast.158), kind=kOutput, calls=%fused_computation.194 | convolution fusion | flops 207619072 | bytes 8198144 | tf_op jit(solution)/shard_map/sub | solution.py:191
  168.3 4.7 %fusion.27 = bf16[12,64,128]{2,1,0:T(8,128)(2,1)S(1)} fusion(bf16[1024,12,64]{0,2,1:T(8,128)(2,1)} %bitcast.171, f32[12,128,1024]{2,1,0:T(8,128)} %get-tuple-element.67, f32[12,128]{1,0:T(8,128)S(1)} %get-tuple-element.66), kind=kOutput, calls=%fused_computation.69 | convolution fusion | flops 204570624 | bytes 8067072 | tf_op jit(solution)/shard_map/hqk,khd->qhd/dot_general | solution.py:194
  177.5 3.7 convert_reduce_fusion.3
  186.3 5.3 %bitcast_convert_fusion = (bf16[1024,12,64]{0,2,1:T(8,128)(2,1)S(1)}, f32[12,64,1024]{2,1,0:T(8,128)}) fusion(bf16[128,12,64]{0,2,1:T(8,128)(2,1)} %bitcast.185, f32[12,128,1024]{2,1,0:T(8,128)} %get-tuple-element.67, f32[12,128]{1,0:T(8,128)} %copy-done.24), kind=kOutput, calls=%fused_computation.26 | convolution fusion | flops 205258752 | bytes 11212800 | tf_op jit(solution)/shard_map/hqk,qhd->khd/dot_general | solution.py:243
  191.6 3.7 multiply_reduce_fusion
  204.6 5.5 %fusion.11 = f32[768,1536]{1,0:T(8,128)} fusion(bf16[1024,768]{1,0:T(8,128)(2,1)S(1)} %copy-done.11, bf16[1024,768]{0,1:T(8,128)(2,1)S(1)} %bitcast.200, bf16[1024,768]{0,1:T(8,128)(2,1)S(1)} %bitcast.174), kind=kOutput, calls=%fused_computation.44 | convolution fusion | flops 2422210560 | bytes 9437184 | tf_op jit(solution)/shard_map/td,tf->df/dot_general | solution.py:263
  210.1 5.2 %fusion.46 = f32[3072,768]{1,0:T(8,128)} fusion(bf16[1,1,128,768]{3,2,1,0:T(8,128)(2,1)S(1)} %copy-done.15, f32[128,3072]{1,0:T(8,128)S(1)} %copy-done.7), kind=kOutput, calls=%fused_computation.118 | convolution fusion | flops 607518720 | bytes 11206656 | tf_op jit(solution)/shard_map/tf,td->fd/dot_general | solution.py:208
  233.0 8.3 %pad_maximum_fusion = f32[768,3072]{1,0:T(8,128)} fusion(f32[768,768]{1,0:T(8,128)S(1)} %fusion.59, f32[768,1536]{1,0:T(8,128)} %fusion.11, f32[768,768]{1,0:T(8,128)} %fusion.49), kind=kLoop, calls=%fused_computation.1 | loop fusion | flops 4718592 | bytes 18874368 | tf_op jit(solution)/shard_map/concatenate | solution.py:264
  244.1 4.1 dynamic-slice_convert_fusion.1
  260.3 5.2 %collective-permute-done.11 = bf16[128,768]{1,0:T(8,128)(2,1)S(1)} collective-permute-done((bf16[128,768]{1,0:T(8,128)(2,1)S(1)}, bf16[128,768]{1,0:T(8,128)(2,1)S(1)}, u32[]{:S(2)}, u32[]{:S(2)}) %collective-permute-start.11) | collective-permute-done | bytes 196640 | tf_op jit(solution)/shard_map/ppermute | solution.py:25
  279.2 7.1 %all-to-all-start = ((f32[64,8,256]{2,1,0:T(8,128)}), f32[64,8,256]{2,1,0:T(8,128)}, u32[]{:S(2)}, u32[]{:S(2)}) async-start(f32[64,8,256]{2,1,0:T(8,128)} %pad_maximum_fusion.6), calls=%async_computation | async-start | bytes 1048576 | tf_op jit(solution)/shard_map/all_to_all | solution.py:282
  286.3 5.3 %add_convert_fusion = bf16[768,1536]{1,0:T(8,128)(2,1)} fusion(bf16[768,1536]{1,0:T(8,128)(2,1)} %collective-permute-done.17, f32[768,3072]{1,0:T(8,128)} %pad_maximum_fusion, s32[]{:T(128)S(6)} %select_n.235), kind=kLoop, calls=%fused_computation.14 | loop fusion | flops 3538944 | bytes 9437188 | tf_op jit(solution)/shard_map/convert_element_type | solution.py:115
  291.6 4.9 %convert_element_type.220 = bf16[32,24,2,2,384]{4,3,2,1,0:T(2,128)(2,1)S(1)} reshape(bf16[768,1536]{1,0:T(8,128)(2,1)} %add_convert_fusion) | data formatting | bytes 4718592 | tf_op jit(solution)/shard_map/convert_element_type | solution.py:115
  298.4 9.7 %all-to-all-start.2 = ((bf16[64,48,384]{2,1,0:T(8,128)(2,1)}), bf16[64,48,384]{2,1,0:T(8,128)(2,1)S(1)}, u32[]{:S(2)}, u32[]{:S(2)}) async-start(bf16[64,48,384]{2,1,0:T(8,128)(2,1)} %bitcast.150), calls=%async_computation.2 | async-start | bytes 4718592 | tf_op jit(solution)/shard_map/all_to_all | solution.py:115
  308.2 3.6 add_convert_fusion.1
  313.4 5.2 %add_convert_fusion.2 = bf16[768,1536]{1,0:T(8,128)(2,1)} fusion(bf16[768,1536]{1,0:T(8,128)(2,1)} %collective-permute-done.15, f32[768,3072]{1,0:T(8,128)} %copy-done, s32[]{:T(128)S(6)} %select_n.235), kind=kLoop, calls=%fused_computation.16 | loop fusion | flops 3538944 | bytes 9437188 | tf_op jit(solution)/shard_map/convert.15
  318.6 5.9 %reshape.478 = bf16[32,24,2,2,384]{4,3,2,1,0:T(2,128)(2,1)} reshape(bf16[768,1536]{1,0:T(8,128)(2,1)} %add_convert_fusion.2) | data formatting | bytes 4718592 | tf_op jit(solution)/shard_map/reshape | solution.py:120
  329.5 9.0 %all-to-all-done.2 = bf16[64,48,384]{2,1,0:T(8,128)(2,1)S(1)} async-done(((bf16[64,48,384]{2,1,0:T(8,128)(2,1)}), bf16[64,48,384]{2,1,0:T(8,128)(2,1)S(1)}, u32[]{:S(2)}, u32[]{:S(2)}) %all-to-all-start.2) | async-done | bytes 2359328 | tf_op jit(solution)/shard_map/all_to_all | solution.py:115
  338.5 6.8 %all-to-all-start.1 = ((bf16[64,96,384]{2,1,0:T(8,128)(2,1)}), bf16[64,96,384]{2,1,0:T(8,128)(2,1)}, u32[]{:S(2)}, u32[]{:S(2)}) async-start(bf16[64,96,384]{2,1,0:T(8,128)(2,1)} %pad_maximum_fusion.1), calls=%async_computation.1 | async-start | bytes 9437184 | tf_op jit(solution)/shard_map/all_to_all | solution.py:115
  346.0 6.8 %fusion.31 = bf16[1,1,128,768]{3,2,1,0:T(8,128)(2,1)} fusion(f32[128,768]{1,0:T(8,128)S(1)} %get-tuple-element.69, bf16[3072,384]{1,0:T(8,128)(2,1)} %bitcast.163, bf16[3072,384]{1,0:T(8,128)(2,1)} %bitcast.161, pred[]{:T(512)S(6)} %eq.41, f32[768]{0:T(1024)S(1)} %copy-done.30, f32[128,3072]{1,0:T(8,128)} %copy-done.6), kind=kOutput, calls=%fused_computation.72 | convolution fusion | flops 629047296 | bytes 6884353 | tf_op jit(solution)/shard_map/dot_general | solution.py:203
  358.7 40.6 %all-to-all-done.1 = bf16[64,96,384]{2,1,0:T(8,128)(2,1)} async-done(((bf16[64,96,384]{2,1,0:T(8,128)(2,1)}), bf16[64,96,384]{2,1,0:T(8,128)(2,1)}, u32[]{:S(2)}, u32[]{:S(2)}) %all-to-all-start.1) | async-done | bytes 4718624 | tf_op jit(solution)/shard_map/all_to_all | solution.py:115
  402.4 4.9 %collective-permute-start.18 = (bf16[72,384]{1,0:T(8,128)(2,1)S(1)}, bf16[72,384]{1,0:T(8,128)(2,1)S(1)}, u32[]{:S(2)}, u32[]{:S(2)}) collective-permute-start(bf16[72,384]{1,0:T(8,128)(2,1)S(1)} %pad_maximum_fusion.8), channel_id=1, source_target_pairs={{0,1},{1,0},{2,3},{3,2},{4,5},{5,4},{6,7},{7,6},{8,9},{9,8},{10,11... | collective-permute-start | bytes 165896 | tf_op jit(solution)/shard_map/ppermute | solution.py:34
  409.1 3.5 collective-permute-done.19
  (256 shorter events, 140.0 us)
Async XLA Ops:
  7.2 90.0 %all-gather.2.cloned.1.call-start = ((), (), s32[]{:S(2)}) async-start(), calls=%async_computation.3 | async-start | bytes 7729152 | tf_op jit(solution)/shard_map/all_gather | solution.py:92
  8.0 11.2 %collective-permute-start.6 = (bf16[48,384]{1,0:T(8,128)(2,1)S(1)}, bf16[48,384]{1,0:T(8,128)(2,1)S(1)}, u32[]{:S(2)}, u32[]{:S(2)}) collective-permute-start(bf16[48,384]{1,0:T(8,128)(2,1)S(1)} %get-tuple-element.59), channel_id=1, source_target_pairs={{0,1},{1,0},{2,3},{3,2},{4,5},{5,4},{6,7},{7,6},{8,9},{9,8},{10,11... | collective-permute-start | bytes 110600 | tf_op jit(solution)/shard_map/ppermute | solution.py:34
  19.0 2.9 collective-permute-start.4
  19.2 4.5 %collective-permute-start.7 = (bf16[96,384]{1,0:T(8,128)(2,1)S(1)}, bf16[96,384]{1,0:T(8,128)(2,1)S(1)}, u32[]{:S(2)}, u32[]{:S(2)}) collective-permute-start(bf16[96,384]{1,0:T(8,128)(2,1)S(1)} %maximum_select_fusion.8), channel_id=1, source_target_pairs={{0,66},{64,2},{2,64},{66,0},{1,67},{65,3},{3,65},{67,1},{4,70},{68... | collective-permute-start | bytes 221192 | tf_op jit(solution)/shard_map/ppermute | solution.py:30
  21.9 6.0 %collective-permute-start.5 = (bf16[24,3200]{1,0:T(8,128)(2,1)S(1)}, bf16[24,3200]{1,0:T(8,128)(2,1)S(1)}, u32[]{:S(2)}, u32[]{:S(2)}) collective-permute-start(bf16[24,3200]{1,0:T(8,128)(2,1)S(1)} %maximum_select_fusion.5), channel_id=1, source_target_pairs={{0,66},{64,2},{2,64},{66,0},{1,67},{65,3},{3,65},{67,1},{4,70},{68... | collective-permute-start | bytes 460808 | tf_op jit(solution)/shard_map/ppermute | solution.py:30
  28.9 73.9 %copy-start.12 = (bf16[1,1,128,768]{3,2,1,0:T(8,128)(2,1)S(1)}, bf16[1,1,128,768]{3,2,1,0:T(8,128)(2,1)}, u32[]{:S(2)}) copy-start(bf16[1,1,128,768]{3,2,1,0:T(8,128)(2,1)} %param.15) | copy-start | bytes 589828
  102.1 41.7 %collective-permute-start.8 = (bf16[768,3072]{1,0:T(8,128)(2,1)}, bf16[768,3072]{1,0:T(8,128)(2,1)}, u32[]{:S(2)}, u32[]{:S(2)}) collective-permute-start(bf16[768,3072]{1,0:T(8,128)(2,1)} %slice.222), channel_id=1, source_target_pairs={{0,1},{1,0},{2,3},{3,2},{4,5},{5,4},{6,7},{7,6},{8,9},{9,8},{10,11... | collective-permute-start | bytes 14155784 | tf_op jit(solution)/shard_map/ppermute | solution.py:34
  102.7 8.0 %collective-permute-start.1 = (bf16[128,768]{1,0:T(8,128)(2,1)S(1)}, bf16[128,768]{1,0:T(8,128)(2,1)S(1)}, u32[]{:S(2)}, u32[]{:S(2)}) collective-permute-start(bf16[128,768]{1,0:T(8,128)(2,1)S(1)} %bitcast.165), channel_id=1, source_target_pairs={{0,2},{64,66},{2,0},{66,64},{1,3},{65,67},{3,1},{67,65},{4,6},{68,... | collective-permute-start | bytes 589832 | tf_op jit(solution)/shard_map/ppermute | solution.py:25
  105.4 9.9 %collective-permute-start = (bf16[128,768]{1,0:T(8,128)(2,1)S(1)}, bf16[128,768]{1,0:T(8,128)(2,1)S(1)}, u32[]{:S(2)}, u32[]{:S(2)}) collective-permute-start(bf16[128,768]{1,0:T(8,128)(2,1)S(1)} %bitcast.166), channel_id=1, source_target_pairs={{0,64},{64,2},{2,66},{66,0},{1,65},{65,3},{3,67},{67,1},{4,68},{68... | collective-permute-start | bytes 589832 | tf_op jit(solution)/shard_map/ppermute | solution.py:25
  105.7 9.6 %collective-permute-start.2 = (bf16[128,768]{1,0:T(8,128)(2,1)S(1)}, bf16[128,768]{1,0:T(8,128)(2,1)S(1)}, u32[]{:S(2)}, u32[]{:S(2)}) collective-permute-start(bf16[128,768]{1,0:T(8,128)(2,1)S(1)} %bitcast.167), channel_id=1, source_target_pairs={{0,66},{64,0},{2,64},{66,2},{1,67},{65,1},{3,65},{67,3},{4,70},{68... | collective-permute-start | bytes 589832 | tf_op jit(solution)/shard_map/ppermute | solution.py:25
  116.3 4.9 %collective-permute-start.3 = (bf16[4,128,768]{2,1,0:T(8,128)(2,1)}, bf16[4,128,768]{2,1,0:T(8,128)(2,1)S(1)}, u32[]{:S(2)}, u32[]{:S(2)}) collective-permute-start(bf16[4,128,768]{2,1,0:T(8,128)(2,1)} %pad_maximum_fusion.5), channel_id=1, source_target_pairs={{0,1},{1,0},{2,3},{3,2},{4,5},{5,4},{6,7},{7,6},{8,9},{9,8},{10,11... | collective-permute-start | bytes 2359304 | tf_op jit(solution)/shard_map/ppermute | solution.py:34
  120.9 16.9 %collective-permute-start.9 = (bf16[768,1536]{1,0:T(8,128)(2,1)}, bf16[768,1536]{1,0:T(8,128)(2,1)}, u32[]{:S(2)}, u32[]{:S(2)}) collective-permute-start(bf16[768,1536]{1,0:T(8,128)(2,1)} %slice.235), channel_id=1, source_target_pairs={{0,1},{1,0},{2,3},{3,2},{4,5},{5,4},{6,7},{7,6},{8,9},{9,8},{10,11... | collective-permute-start | bytes 7077896 | tf_op jit(solution)/shard_map/ppermute | solution.py:34
  153.2 9.9 %copy-start.16 = (bf16[128,768]{0,1:T(8,128)(2,1)}, bf16[128,768]{0,1:T(8,128)(2,1)S(1)}, u32[]{:S(2)}) copy-start(bf16[128,768]{0,1:T(8,128)(2,1)S(1)} %copy.221) | copy-start | bytes 589828
  163.2 9.9 %slice-start.2 = ((s8[4718592]{0:T(1024)(128)(4,1)}), s8[524288]{0:T(1024)(128)(4,1)S(1)}, s32[]{:S(2)}) async-start(s8[4718592]{0:T(1024)(128)(4,1)} %bitcast.146), calls=%async_computation.6 | async-start | bytes 1048576
  174.5 9.2 %copy-start.26 = (f32[128]{0:T(128)}, f32[128]{0:T(128)S(1)}, u32[]{:S(2)}) copy-start(f32[128]{0:T(128)S(1)} %broadcast_multiply_fusion.5) | copy-start | bytes 1540
  174.7 9.0 %copy-start.28 = (f32[128]{0:T(128)}, f32[128]{0:T(128)S(1)}, u32[]{:S(2)}) copy-start(f32[128]{0:T(128)S(1)} %add_rsqrt_fusion.1) | copy-start | bytes 1540
  186.3 9.1 %slice-start.6 = ((s8[6291456]{0:T(1024)(128)(4,1)}), s8[4194304]{0:T(1024)(128)(4,1)S(1)}, s32[]{:S(2)}) async-start(s8[6291456]{0:T(1024)(128)(4,1)} %bitcast.156), calls=%async_computation.10 | async-start | bytes 8388608
  227.2 25.0 %collective-permute-start.10 = (bf16[4,128,768]{2,1,0:T(8,128)(2,1)}, bf16[4,128,768]{2,1,0:T(8,128)(2,1)}, u32[]{:S(2)}, u32[]{:S(2)}) collective-permute-start(bf16[4,128,768]{2,1,0:T(8,128)(2,1)} %bitcast.183), channel_id=1, source_target_pairs={{0,1},{1,0},{2,3},{3,2},{4,5},{5,4},{6,7},{7,6},{8,9},{9,8},{10,11... | collective-permute-start | bytes 2359304 | tf_op jit(solution)/shard_map/ppermute | solution.py:34
  244.0 42.3 %collective-permute-start.17 = (bf16[768,1536]{1,0:T(8,128)(2,1)S(1)}, bf16[768,1536]{1,0:T(8,128)(2,1)}, u32[]{:S(2)}, u32[]{:S(2)}) collective-permute-start(bf16[768,1536]{1,0:T(8,128)(2,1)S(1)} %dynamic-slice_convert_fusion), channel_id=1, source_target_pairs={{0,1},{1,0},{2,3},{3,2},{4,5},{5,4},{6,7},{7,6},{8,9},{9,8},{10,11... | collective-permute-start | bytes 7077896 | tf_op jit(solution)/shard_map/ppermute | solution.py:34
  248.2 60.0 %collective-permute-start.16 = (bf16[3072,384]{1,0:T(8,128)(2,1)}, bf16[3072,384]{1,0:T(8,128)(2,1)}, u32[]{:S(2)}, u32[]{:S(2)}) collective-permute-start(bf16[3072,384]{1,0:T(8,128)(2,1)} %dynamic-slice_convert_fusion.1), channel_id=1, source_target_pairs={{0,1},{1,0},{2,3},{3,2},{4,5},{5,4},{6,7},{7,6},{8,9},{9,8},{10,11... | collective-permute-start | bytes 7077896 | tf_op jit(solution)/shard_map/ppermute | solution.py:34
  250.3 20.3 %copy-start = (f32[768,3072]{1,0:T(8,128)}, f32[768,3072]{1,0:T(8,128)S(1)}, u32[]{:S(2)}) copy-start(f32[768,3072]{1,0:T(8,128)S(1)} %fusion.66) | copy-start | bytes 28311556
  254.8 10.8 %collective-permute-start.11 = (bf16[128,768]{1,0:T(8,128)(2,1)S(1)}, bf16[128,768]{1,0:T(8,128)(2,1)S(1)}, u32[]{:S(2)}, u32[]{:S(2)}) collective-permute-start(bf16[128,768]{1,0:T(8,128)(2,1)S(1)} %get-tuple-element.46), channel_id=1, source_target_pairs={{0,66},{64,0},{2,64},{66,2},{1,67},{65,1},{3,65},{67,3},{4,70},{68... | collective-permute-start | bytes 589832 | tf_op jit(solution)/shard_map/ppermute | solution.py:25
  257.3 11.6 %collective-permute-start.13 = (bf16[128,768]{1,0:T(8,128)(2,1)S(1)}, bf16[128,768]{1,0:T(8,128)(2,1)S(1)}, u32[]{:S(2)}, u32[]{:S(2)}) collective-permute-start(bf16[128,768]{1,0:T(8,128)(2,1)S(1)} %get-tuple-element.47), channel_id=1, source_target_pairs={{0,64},{64,2},{2,66},{66,0},{1,65},{65,3},{3,67},{67,1},{4,68},{68... | collective-permute-start | bytes 589832 | tf_op jit(solution)/shard_map/ppermute | solution.py:25
  257.3 11.6 %collective-permute-start.12 = (bf16[128,768]{1,0:T(8,128)(2,1)S(1)}, bf16[128,768]{1,0:T(8,128)(2,1)S(1)}, u32[]{:S(2)}, u32[]{:S(2)}) collective-permute-start(bf16[128,768]{1,0:T(8,128)(2,1)S(1)} %get-tuple-element.48), channel_id=1, source_target_pairs={{0,2},{64,66},{2,0},{66,64},{1,3},{65,67},{3,1},{67,65},{4,6},{68,... | collective-permute-start | bytes 589832 | tf_op jit(solution)/shard_map/ppermute | solution.py:25
  265.6 47.8 %collective-permute-start.15 = (bf16[768,1536]{1,0:T(8,128)(2,1)}, bf16[768,1536]{1,0:T(8,128)(2,1)}, u32[]{:S(2)}, u32[]{:S(2)}) collective-permute-start(bf16[768,1536]{1,0:T(8,128)(2,1)} %dynamic-slice_convert_fusion.2), channel_id=1, source_target_pairs={{0,1},{1,0},{2,3},{3,2},{4,5},{5,4},{6,7},{7,6},{8,9},{9,8},{10,11... | collective-permute-start | bytes 7077896 | tf_op jit(solution)/shard_map/ppermute | solution.py:34
  279.2 19.2 %all-to-all-start = ((f32[64,8,256]{2,1,0:T(8,128)}), f32[64,8,256]{2,1,0:T(8,128)}, u32[]{:S(2)}, u32[]{:S(2)}) async-start(f32[64,8,256]{2,1,0:T(8,128)} %pad_maximum_fusion.6), calls=%async_computation | async-start | bytes 1048576 | tf_op jit(solution)/shard_map/all_to_all | solution.py:282
  298.4 40.1 %all-to-all-start.2 = ((bf16[64,48,384]{2,1,0:T(8,128)(2,1)}), bf16[64,48,384]{2,1,0:T(8,128)(2,1)S(1)}, u32[]{:S(2)}, u32[]{:S(2)}) async-start(bf16[64,48,384]{2,1,0:T(8,128)(2,1)} %bitcast.150), calls=%async_computation.2 | async-start | bytes 4718592 | tf_op jit(solution)/shard_map/all_to_all | solution.py:115
  329.5 16.5 %copy-start.30 = (f32[768]{0:T(1024)S(1)}, f32[768]{0:T(1024)}, u32[]{:S(2)}) copy-start(f32[768]{0:T(1024)} %get-tuple-element.24) | copy-start | bytes 9220
  338.5 60.8 %all-to-all-start.1 = ((bf16[64,96,384]{2,1,0:T(8,128)(2,1)}), bf16[64,96,384]{2,1,0:T(8,128)(2,1)}, u32[]{:S(2)}, u32[]{:S(2)}) async-start(bf16[64,96,384]{2,1,0:T(8,128)(2,1)} %pad_maximum_fusion.1), calls=%async_computation.1 | async-start | bytes 9437184 | tf_op jit(solution)/shard_map/all_to_all | solution.py:115
  353.9 3.6 collective-permute-start.14
  402.4 5.8 %collective-permute-start.18 = (bf16[72,384]{1,0:T(8,128)(2,1)S(1)}, bf16[72,384]{1,0:T(8,128)(2,1)S(1)}, u32[]{:S(2)}, u32[]{:S(2)}) collective-permute-start(bf16[72,384]{1,0:T(8,128)(2,1)S(1)} %pad_maximum_fusion.8), channel_id=1, source_target_pairs={{0,1},{1,0},{2,3},{3,2},{4,5},{5,4},{6,7},{7,6},{8,9},{9,8},{10,11... | collective-permute-start | bytes 165896 | tf_op jit(solution)/shard_map/ppermute | solution.py:34
  408.2 4.4 %collective-permute-start.19 = (bf16[1,2,72,384]{3,2,1,0:T(8,128)(2,1)S(1)}, bf16[1,2,72,384]{3,2,1,0:T(8,128)(2,1)S(1)}, u32[]{:S(2)}, u32[]{:S(2)}) collective-permute-start(bf16[1,2,72,384]{3,2,1,0:T(8,128)(2,1)S(1)} %maximum_select_fusion.7), channel_id=1, source_target_pairs={{0,64},{64,0},{1,65},{65,1},{2,66},{66,2},{3,67},{67,3},{4,68},{68... | collective-permute-start | bytes 331784 | tf_op jit(solution)/shard_map/ppermute | solution.py:297
  (34 other events, 146.7 us)
Sparse Core Ops, SparseCore 0:
  29.0 68.1 all-gather.1

commit v2 on v1

v2 whole, which is shorter than its diff:
```python
import jax
import jax.numpy as jnp
from jax import lax
from jax.experimental import pallas as pl
from jax.experimental.pallas import tpu as pltpu
from jax.sharding import Mesh, PartitionSpec as P

HEAD_DIM = 64
HEADS = 12
WIDTH = 768
HIDDEN = 3072
TOK = 128
RING = ("xl", "xh")
CHIPS = ("xl", "z", "y", "xh")
SHARD = ("z", "y", "xh", "c")
SWAP = [(0, 1), (1, 0)]
F32 = jnp.float32
BF16 = jnp.bfloat16


def ring_index(place):
    return (place % 2) * 2 + place // 2


def ring_shift(value, steps):
    pairs = [(ring_index(i), ring_index((i + steps) % 4)) for i in range(4)]
    return lax.ppermute(value, RING, pairs)


def mirror(value):
    pairs = [(ring_index(i), ring_index(3 - i)) for i in range(4)]
    return lax.ppermute(value, RING, pairs)


def core_swap(value):
    return lax.ppermute(value, "c", SWAP)


def ordered(flag, own, other, axis):
    return jnp.where(
        flag == 0,
        jnp.concatenate([own, other], axis=axis),
        jnp.concatenate([other, own], axis=axis),
    )


def half_of(value, which, axis):
    size = value.shape[axis] // 2
    return lax.dynamic_slice_in_dim(value, which * size, size, axis)


def normed_of(values):
    average = jnp.mean(values, axis=-1, keepdims=True)
    centered = values - average
    inverse = lax.rsqrt(jnp.mean(centered * centered, axis=-1, keepdims=True) + 1e-05)
    return centered * inverse, inverse


def norm_backward(upstream, normed, inverse, norm_gain):
    scaled = upstream * norm_gain
    return inverse * (
        scaled
        - jnp.mean(scaled, axis=-1, keepdims=True)
        - normed * jnp.mean(scaled * normed, axis=-1, keepdims=True)
    )


def gather_tokens(own):
    ring = jnp.stack([own] + [ring_shift(own, steps) for steps in (1, 2, 3)])
    return jnp.concatenate([ring, core_swap(ring)])


VMEM_LIMIT = 56 * 1024 * 1024


def dot(a, b, dims=((1,), (0,))):
    return lax.dot_general(a, b, (dims, ((), ())), preferred_element_type=F32)


ROWS = ((1,), (1,))


def call(kernel, outs, scratch, specs, args, flops, size):
    return pl.pallas_call(
        kernel,
        out_shape=[jax.ShapeDtypeStruct(shape, kind) for shape, kind in outs],
        in_specs=specs,
        scratch_shapes=scratch,
        compiler_params=pltpu.CompilerParams(vmem_limit_bytes=VMEM_LIMIT),
        cost_estimate=pl.CostEstimate(flops=flops, bytes_accessed=size, transcendentals=0),
    )(*args)


IN_VMEM = pl.BlockSpec(memory_space=pltpu.VMEM)
IN_SMEM = pl.BlockSpec(memory_space=pltpu.SMEM)
ANYWHERE = pl.BlockSpec(memory_space=pl.ANY)


def stacked_heads(pair):
    lane = lax.broadcasted_iota(jnp.int32, pair.shape, 1)
    zero = jnp.zeros_like(pair)
    return jnp.concatenate([jnp.where(lane < 64, pair, zero), jnp.where(lane < 64, zero, pair)])


def merged_heads(rows):
    lane = lax.broadcasted_iota(jnp.int32, (128, 128), 1)
    return jnp.where(lane < 64, rows[:128], rows[128:])


def front_kernel(
    meta, tok, vec, mine, other, h1, q, k, v, p, o, mid, weights, bias, sems
):
    core = meta[0]
    copies = []
    for b in range(2):
        cols = pl.ds(b * WIDTH, WIDTH)
        copies.append(pltpu.make_async_copy(mine.at[:, :, cols], weights.at[2 * core + b], sems.at[b]))
        copies.append(
            pltpu.make_async_copy(other.at[:, :, cols], weights.at[2 * (1 - core) + b], sems.at[2 + b])
        )
    for copy in copies:
        copy.start()
    for j in range(8):
        unit, _ = normed_of(tok[j].astype(F32))
        h1[j * TOK : (j + 1) * TOK, :] = (unit * vec[0:1, :] + vec[1:2, :]).astype(BF16)
    key_row = lax.broadcasted_iota(jnp.int32, (TOK, 2 * TOK), 0)
    query_col = lax.broadcasted_iota(jnp.int32, (TOK, 2 * TOK), 1) % TOK
    bias[0:TOK, :] = jnp.where(key_row <= query_col, 0.0, -1e30)
    for j in range(1, 8):
        shown = meta[j] > 0
        bias[j * TOK : (j + 1) * TOK, :] = jnp.full((TOK, 2 * TOK), jnp.where(shown, 0.0, -1e30), F32)
    for copy in copies:
        copy.wait()
    q[...] = (dot(h1[0:TOK, :], weights[0].reshape(WIDTH, WIDTH)) + vec[2:3, :]).astype(BF16)
    weight_key = weights[1].reshape(WIDTH, WIDTH)
    weight_value = weights[2].reshape(WIDTH, WIDTH)
    for j in range(4):
        rows = slice(j * 256, (j + 1) * 256)
        k[rows, :] = dot(h1[rows, :], weight_key).astype(BF16)
        v[rows, :] = (dot(h1[rows, :], weight_value) + vec[3:4, :]).astype(BF16)
    for pair in range(6):
        lanes = slice(pair * 128, (pair + 1) * 128)
        scores = dot(k[:, lanes], stacked_heads(q[:, lanes]), ROWS) * 0.125 + bias[...]
        exponent = jnp.exp(scores - jnp.max(scores, axis=0, keepdims=True))
        probs = exponent * (1.0 / jnp.sum(exponent, axis=0, keepdims=True))
        low = probs.astype(BF16)
        p[pair] = low
        attended = dot(v[:, lanes].T, low)
        o[:, lanes] = merged_heads(attended.T).astype(BF16)
    mid[...] = (
        tok[0].astype(F32) + dot(o[...], weights[3].reshape(WIDTH, WIDTH)) + vec[4:5, :]
    )


def middle_kernel(
    meta, mid, dy, vec, bias_up, mine, other_first, other_rest,
    result, act, du_keep, du_send, h2, dmid, da, dattended, small, up_bias_grad,
    up, down, weight_out, sems,
):
    core = meta[0]
    far = 1 - core
    copies = [
        pltpu.make_async_copy(mine.at[:, :, pl.ds(1536, 1536)], up.at[core], sems.at[0]),
        pltpu.make_async_copy(other_rest.at[:, :, pl.ds(0, 1536)], up.at[far], sems.at[1]),
    ]
    for g in range(4):
        copies.append(
            pltpu.make_async_copy(
                mine.at[:, :, pl.ds(3072 + 384 * g, 384)], down.at[core, :, g], sems.at[2 + g]
            )
        )
        copies.append(
            pltpu.make_async_copy(
                other_rest.at[:, :, pl.ds(1536 + 384 * g, 384)], down.at[far, :, g], sems.at[6 + g]
            )
        )
    for copy in copies:
        copy.start()

    @pl.when(core == 0)
    def _():
        copy = pltpu.make_async_copy(other_first.at[:, :, pl.ds(768, 768)], weight_out, sems.at[10])
        copy.start()
        copy.wait()

    @pl.when(core == 1)
    def _():
        copy = pltpu.make_async_copy(mine.at[:, :, pl.ds(768, 768)], weight_out, sems.at[10])
        copy.start()
        copy.wait()

    unit, inverse = normed_of(mid[...])
    h2[...] = (unit * vec[5:6, :] + vec[6:7, :]).astype(BF16)
    for copy in copies:
        copy.wait()
    low = dy[...]
    outcome = [mid[:, 384 * n : 384 * n + 384] + vec[7:8, 384 * n : 384 * n + 384] for n in range(2)]
    dh2 = None
    for half in range(2):
        cols = slice(half * 1536, (half + 1) * 1536)
        wide = up[half].reshape(WIDTH, 1536)
        u = dot(h2[...], wide) + bias_up[:, cols]
        cube = 0.7978845608028654 * (u + 0.044715 * u * u * u)
        tanh = jnp.tanh(cube)
        low_act = (0.5 * u * (1.0 + tanh)).astype(BF16)
        act[:, cols] = low_act
        slope_half = 0.5 * (1.0 + tanh) + 0.5 * u * (1.0 - tanh * tanh) * 0.7978845608028654 * (
            1.0 + 3.0 * 0.044715 * u * u
        )
        grad_act = None
        for n in range(2):
            rows = down[n, half * 8 : half * 8 + 8].reshape(1536, 384)
            outcome[n] = outcome[n] + dot(low_act, rows)
            term = dot(low[:, 384 * n : 384 * n + 384], rows, ROWS)
            grad_act = term if grad_act is None else grad_act + term
        du = (grad_act * slope_half).astype(BF16)
        up_bias_grad[:, cols] = jnp.sum(du.astype(F32), axis=0, keepdims=True)

        @pl.when(core == half)
        def _():
            du_keep[...] = du

        @pl.when(core != half)
        def _():
            du_send[...] = du

        term = dot(du, wide, ROWS)
        dh2 = term if dh2 is None else dh2 + term
    for n in range(2):
        result[:, 384 * n : 384 * n + 384] = outcome[n].astype(BF16)
    upstream = low.astype(F32)
    dm = upstream + norm_backward(dh2, unit, inverse, vec[5:6, :])
    dmid[...] = dm
    branch = dm.astype(BF16)
    da[...] = branch
    small[0:1, :] = jnp.sum(branch.astype(F32), axis=0, keepdims=True)
    small[1:2, :] = jnp.sum(dh2 * unit, axis=0, keepdims=True)
    small[2:3, :] = jnp.sum(dh2, axis=0, keepdims=True)
    small[3:4, :] = jnp.sum(upstream, axis=0, keepdims=True)
    dattended[...] = dot(branch, weight_out[...].reshape(WIDTH, WIDTH), ROWS).astype(BF16)


def attention_back_kernel(meta, q, k, v, p, do, dq, keep, send, value_bias):
    first = meta[0] == 0
    for pair in range(6):
        lanes = slice(pair * 128, (pair + 1) * 128)
        upstream = stacked_heads(do[:, lanes])
        keys = k[:, lanes]
        low = p[pair]
        probs = low.astype(F32)
        dprobs = dot(v[:, lanes], upstream, ROWS)
        inner = jnp.sum(probs * dprobs, axis=0, keepdims=True)
        dscores = (probs * (dprobs - inner)).astype(BF16)
        dk = dot(dscores, stacked_heads(q[:, lanes])) * 0.125
        dv = dot(low, upstream)
        dq[:, lanes] = (merged_heads(dot(keys.T, dscores).T) * 0.125).astype(BF16)
        value_bias[:, lanes] = jnp.sum(dv, axis=0, keepdims=True)
        keep[:, lanes] = jnp.where(first, dk, dv).astype(BF16)
        send[:, lanes] = jnp.where(first, dv, dk).astype(BF16)


def feed_grads_kernel(h2, h2_far, du, du_far, act, act_far, dy, dy_far, out):
    lhs = jnp.concatenate([h2[...], h2_far[...]]).T
    for x in range(4):
        cols = slice(x * 384, (x + 1) * 384)
        grad = dot(lhs, jnp.concatenate([du[:, cols], du_far[:, cols]])).astype(BF16)
        for zy in range(16):
            out[((x % 2) * 16 + zy) * 2 + x // 2, 0:48, :] = grad[zy * 48 : zy * 48 + 48]
    rhs = jnp.concatenate([dy[...], dy_far[...]])
    for part in range(4):
        cols = slice(part * 768, (part + 1) * 768)
        lhs = jnp.concatenate([act[:, cols], act_far[:, cols]]).T
        grad = dot(lhs, rhs).astype(BF16)
        for n in range(16):
            zy, x = part * 4 + n // 4, n % 4
            out[((x % 2) * 16 + zy) * 2 + x // 2, 48:96, :] = grad[n * 48 : n * 48 + 48]


def in_grads_kernel(
    meta, h1, keep, got, o, o_far, da, da_far, dq, dq_far, mine, other,
    out, ring, send, total, weight, weight_query, sems,
):
    core = meta[0]

    def load(source_q, source_kv):
        copies = [
            pltpu.make_async_copy(source_q.at[:, :, pl.ds(0, 768)], weight_query, sems.at[0]),
            source_kv,
        ]
        for copy in copies:
            copy.start()
        for copy in copies:
            copy.wait()

    @pl.when(core == 0)
    def _():
        load(mine, pltpu.make_async_copy(mine.at[:, :, pl.ds(768, 768)], weight, sems.at[1]))

    @pl.when(core == 1)
    def _():
        load(other, pltpu.make_async_copy(mine.at[:, :, pl.ds(0, 768)], weight, sems.at[1]))

    for j in range(8):
        there = (j + 4) % 8
        total[j * TOK : (j + 1) * TOK, :] = (
            keep[j * TOK : (j + 1) * TOK, :].astype(F32)
            + got[there * TOK : (there + 1) * TOK, :].astype(F32)
        ).astype(BF16)
    whole = weight[...].reshape(WIDTH, WIDTH)
    for j in range(8):
        grad = dot(total[j * TOK : (j + 1) * TOK, :], whole, ROWS)
        if j == 0:
            grad = grad + dot(dq[...], weight_query[...].reshape(WIDTH, WIDTH), ROWS)
        if j < 4:
            ring[j] = grad
        else:
            send[j - 4] = grad.astype(BF16)
    first = core == 0
    lhs = h1[...].T
    lhs_own = jnp.where(
        first,
        jnp.concatenate([h1[0:TOK, :], h1[4 * TOK : 5 * TOK, :]]).astype(F32),
        jnp.concatenate([o[...], o_far[...]]).astype(F32),
    ).astype(BF16).T
    rhs_own = jnp.where(
        first,
        jnp.concatenate([dq[...], dq_far[...]]).astype(F32),
        jnp.concatenate([da[...], da_far[...]]).astype(F32),
    ).astype(BF16)
    for b in range(2):
        cols = slice(b * 384, (b + 1) * 384)
        grad = dot(lhs, total[:, cols]).astype(BF16)
        grad_own = dot(lhs_own, rhs_own[:, cols]).astype(BF16)
        for zy in range(16):
            rows = slice(zy * 48, zy * 48 + 48)
            out[(b * 16 + zy) * 2 + 1 - core] = grad[rows]
            out[(b * 16 + zy) * 2 + core] = grad_own[rows]


def gather_weights(core, xh, pieces):
    in_weight, out_weight, up_weight, down_weight, vectors, up_bias = pieces
    first = jnp.concatenate([in_weight, out_weight], axis=1)
    small = jnp.concatenate(
        [jnp.stack(vectors, axis=1), up_bias.reshape(12, 4), jnp.zeros((12, 116), BF16)], axis=1
    )

    def part(which):
        return jnp.concatenate([half_of(first, which, 1), half_of(up_weight, which, 1), small], axis=1)

    rows = ordered(core, part(core), core_swap(part(1 - core)), 0)
    rows = ordered(xh, rows, mirror(rows), 0)
    down = ordered(core, half_of(down_weight, core, 1), core_swap(half_of(down_weight, 1 - core, 1)), 0)
    down = ordered(xh, down, mirror(down), 0)
    packed = jnp.concatenate(
        [rows[:, :3072]] + [down[48 * k : 48 * k + 48] for k in range(4)] + [rows[:, 3072:]], axis=1
    )
    return lax.all_gather(packed, ("z", "y"), axis=0)


def spread(blocks):
    got = lax.all_to_all(blocks, CHIPS, 0, 0, tiled=True)
    return jnp.sum(got.astype(F32), axis=0)


def local(
    tokens,
    cotangent,
    first_gain,
    first_offset,
    in_weight,
    query_bias,
    value_bias,
    out_weight,
    out_bias,
    second_gain,
    second_offset,
    up_weight,
    up_bias,
    down_weight,
    down_bias,
):
    core = lax.axis_index("c")
    xh = lax.axis_index("xh")
    xl = lax.axis_index("xl")
    place = 2 * xh + xl
    own_tokens = tokens.reshape(TOK, WIDTH)
    group = gather_tokens(own_tokens)
    upstream = cotangent.reshape(TOK, WIDTH)
    upstream_half = half_of(upstream, core, 1)
    upstream_far = core_swap(half_of(upstream, 1 - core, 1))
    vectors = (
        first_gain,
        first_offset,
        query_bias,
        value_bias,
        out_bias,
        second_gain,
        second_offset,
        down_bias,
    )
    mine = gather_weights(core, xh, (in_weight, out_weight, up_weight, down_weight, vectors, up_bias))
    other_first = core_swap(mine[:, :, :1536])
    other_rest = core_swap(mine[:, :, 1536:4608])
    small = mine[:, :, 4608:4620].reshape(WIDTH, 12).astype(F32)
    vec = small[:, :8].T
    bias_up = small[:, 8:].reshape(1, HIDDEN)

    blocks = []
    for other in (0, 1):
        for steps in range(4):
            there = (place + 4 - steps) % 4
            blocks.append(((there // 2) * 2 + (core + other) % 2) * 2 + there % 2)
    meta = jnp.stack([core] + [(b < blocks[0]).astype(jnp.int32) for b in blocks[1:]])

    wide = (16, 48, WIDTH)
    h1, query, key, value, probs, attended, middle = call(
        front_kernel,
        [
            ((8 * TOK, WIDTH), BF16),
            ((TOK, WIDTH), BF16),
            ((8 * TOK, WIDTH), BF16),
            ((8 * TOK, WIDTH), BF16),
            ((6, 8 * TOK, 2 * TOK), BF16),
            ((TOK, WIDTH), BF16),
            ((TOK, WIDTH), F32),
        ],
        [
            pltpu.VMEM((4,) + wide, BF16),
            pltpu.VMEM((8 * TOK, 2 * TOK), F32),
            pltpu.SemaphoreType.DMA((4,)),
        ],
        [IN_SMEM, IN_VMEM, IN_VMEM, ANYWHERE, ANYWHERE],
        (meta, group, vec, mine, other_first),
        4_000_000_000,
        20_000_000,
    )
    (
        result,
        act,
        du_keep,
        du_send,
        h2,
        grad_middle,
        da,
        grad_attended,
        small_middle,
        grad_up_bias,
    ) = call(
        middle_kernel,
        [
            ((TOK, WIDTH), BF16),
            ((TOK, HIDDEN), BF16),
            ((TOK, HIDDEN // 2), BF16),
            ((TOK, HIDDEN // 2), BF16),
            ((TOK, WIDTH), BF16),
            ((TOK, WIDTH), F32),
            ((TOK, WIDTH), BF16),
            ((TOK, WIDTH), BF16),
            ((8, WIDTH), F32),
            ((1, HIDDEN), F32),
        ],
        [
            pltpu.VMEM((2, 16, 48, 1536), BF16),
            pltpu.VMEM((2, 16, 4, 48, 384), BF16),
            pltpu.VMEM(wide, BF16),
            pltpu.SemaphoreType.DMA((11,)),
        ],
        [IN_SMEM] + [IN_VMEM] * 4 + [ANYWHERE] * 3,
        (meta, middle, upstream, vec, bias_up, mine, other_first, other_rest),
        3_000_000_000,
        20_000_000,
    )
    act_far = core_swap(act)
    du_far = core_swap(du_send)
    rows_far = core_swap(jnp.concatenate([h2, attended, da]))
    (first_blocks,) = call(
        feed_grads_kernel,
        [((64, 96, 384), BF16)],
        [],
        [IN_VMEM] * 8,
        (h2, rows_far[:TOK], du_keep, du_far, act, act_far, upstream_half, upstream_far),
        2_000_000_000,
        10_000_000,
    )
    first_sum = spread(first_blocks)

    grad_query, keep, send, grad_value_bias = call(
        attention_back_kernel,
        [
            ((TOK, WIDTH), BF16),
            ((8 * TOK, WIDTH), BF16),
            ((8 * TOK, WIDTH), BF16),
            ((1, WIDTH), F32),
        ],
        [],
        [IN_SMEM] + [IN_VMEM] * 5,
        (meta, query, key, value, probs, grad_attended),
        3_000_000_000,
        20_000_000,
    )
    got = core_swap(send)
    query_far = core_swap(grad_query)
    second_blocks, ring, ring_send = call(
        in_grads_kernel,
        [
            ((64, 48, 384), BF16),
            ((4, TOK, WIDTH), F32),
            ((4, TOK, WIDTH), BF16),
        ],
        [
            pltpu.VMEM((8 * TOK, WIDTH), BF16),
            pltpu.VMEM(wide, BF16),
            pltpu.VMEM(wide, BF16),
            pltpu.SemaphoreType.DMA((2,)),
        ],
        [IN_SMEM] + [IN_VMEM] * 9 + [ANYWHERE] * 2,
        (
            meta,
            h1,
            keep,
            got,
            attended,
            rows_far[TOK : 2 * TOK],
            da,
            rows_far[2 * TOK :],
            grad_query,
            query_far,
            mine,
            other_first,
        ),
        3_000_000_000,
        20_000_000,
    )
    second_sum = spread(second_blocks)

    ring = ring + core_swap(ring_send).astype(F32)
    grad_normed = ring[0]
    for steps in (1, 2, 3):
        grad_normed = grad_normed + ring_shift(ring[steps].astype(BF16), -steps).astype(F32)
    unit_one, inverse_one = normed_of(own_tokens.astype(F32))
    grad_input = grad_middle + norm_backward(grad_normed, unit_one, inverse_one, vec[0])

    small_grads = jnp.stack(
        [
            jnp.sum(grad_normed * unit_one, axis=0),
            jnp.sum(grad_normed, axis=0),
            jnp.sum(grad_query.astype(F32), axis=0),
            grad_value_bias[0],
            small_middle[0],
            small_middle[1],
            small_middle[2],
            small_middle[3],
        ],
        axis=1,
    )
    small_grads = jnp.concatenate([small_grads, grad_up_bias.reshape(WIDTH, 4)], axis=1)
    small_grads = jnp.pad(small_grads.reshape(32, 2, 144), ((0, 0), (0, 6), (0, 112)))
    small_got = lax.all_to_all(jnp.concatenate([small_grads, small_grads]), CHIPS, 0, 0, tiled=True)
    small_sum = jnp.sum(small_got, axis=0)
    small_sum = small_sum + core_swap(small_sum)
    small_own = lax.dynamic_slice_in_dim(small_sum, core, 1, 0)[0, :144].reshape(12, 12)

    down_sum = first_sum[48:].astype(BF16)
    down_own = ordered(core, down_sum, core_swap(down_sum), 1)
    down_own = jnp.where(xl == core, down_own, lax.ppermute(down_own, "xl", SWAP)).astype(F32)
    sums = jnp.stack([first_sum[:48], second_sum]).astype(BF16)

    def rows_for(steps):
        there = ((place + steps) % 4) // 2
        return lax.dynamic_slice_in_dim(sums, there * 24, 24, 1)

    parts = jnp.stack([rows_for(0)] + [ring_shift(rows_for(steps), steps) for steps in (1, 2, 3)])
    parts = jnp.stack([parts[(place + 4 - source) % 4] for source in range(4)])
    parts = parts.reshape(4, 2, 2, 12, 384)
    keep_rows = lax.dynamic_index_in_dim(parts, core, 2, keepdims=False)
    send_rows = lax.dynamic_index_in_dim(parts, 1 - core, 2, keepdims=False)
    both = ordered(core, keep_rows[None], core_swap(send_rows)[None], 0)
    wide_own = both.transpose(2, 3, 0, 1, 4).reshape(2, 12, 3072).astype(F32)
    return (
        result.reshape(tokens.shape),
        grad_input.astype(BF16).reshape(tokens.shape),
        small_own[:, 0],
        small_own[:, 1],
        wide_own[1][:, : 3 * WIDTH],
        small_own[:, 2],
        small_own[:, 3],
        wide_own[1][:, 3 * WIDTH :],
        small_own[:, 4],
        small_own[:, 5],
        small_own[:, 6],
        wide_own[0],
        small_own[:, 8:].reshape(48),
        down_own,
        small_own[:, 7],
    )


def solution(mesh):
    fine = Mesh(mesh.devices.reshape(2, 4, 4, 2, 2), ("xl", "z", "y", "xh", "c"))
    tok = P(SHARD, "xl", None, None)
    vec = P(SHARD)
    mat = P(SHARD, None)
    return jax.shard_map(
        local,
        mesh=fine,
        in_specs=(tok, tok, vec, vec, mat, vec, vec, mat, vec, vec, vec, mat, vec, mat, vec),
        out_specs=(tok, tok, vec, vec, mat, vec, vec, mat, vec, vec, vec, mat, vec, mat, vec),
        check_vma=False,
    )
```

time: 429 us -> 358 us (0.83)
  matrix products: 61.5 us -> 0 us
  Pallas kernels: 0 us -> 54.3 us
  local copies, waits for them, and re-layouts: 98.7 us -> 50 us
  other arithmetic: 55.1 us -> 12.3 us
  blocking collectives: 0 us -> 18.9 us
  waiting for transfers between devices: 142 us -> 157 us
  starting transfers between devices: 51.1 us -> 44.6 us
    dot_general x20 -> x0, matrix products: 56.3 us -> none  [the longest x1 6.83 us: local(): jnp.dot(activated, weight_down, preferred_element_type=F32)]
    pallas_call x0 -> x5, Pallas kernels: none -> 54.3 us  [call(): pl.pallas_call(kernel, out_shape=[jax.ShapeDtypeStruct(shape, kind) for s...]
    convert_element_type x8 -> x0, local copies, waits for them, and re-layouts: 20 us -> none  [the longest x3 8.58 us: pair_halves(): low = grad.astype(BF16)]
    all_to_all x0 -> x1, blocking collectives: none -> 18.9 us  [local(): lax.all_to_all(jnp.concatenate([small_grads, small_grads]), CHIPS, 0, 0,...]
    reshape x7 -> x1, local copies, waits for them, and re-layouts: 19.1 us -> 0.85 us  [local(): bias_up = small[:, 8:].reshape(1, HIDDEN)]
    all_to_all x3 -> x2, waiting for transfers between devices: 49.6 us -> 64.9 us  [spread(): got = lax.all_to_all(blocks, CHIPS, 0, 0, tiled=True)]
    concatenate x5 -> x1, other arithmetic: 10.9 us -> 0.04 us  [local(): rows_far = core_swap(jnp.concatenate([h2, attended, da]))]
    all_to_all x3 -> x2, starting transfers between devices: 23.6 us -> 13 us  [spread(): got = lax.all_to_all(blocks, CHIPS, 0, 0, tiled=True)]
  transfers between devices with their start and end apart: 24 -> 30, of which waited for: 12 -> 12; matrix products, arithmetic and copies ran while one was open for 28% -> 12% of each run, Pallas kernels for 0% -> 5%
where the time goes in v2:
time: 358 us; the launch traced here: 352 us
  waiting for transfers between devices  157 us (44%)
  Pallas kernels  54.3 us (15%)
  local copies, waits for them, and re-layouts  50 us (14%)
  starting transfers between devices  44.6 us (12%)
  blocking collectives  18.9 us (5%)
  between operations  14.9 us (4%)
  other arithmetic  12.3 us (3%)
    all_gather x1, waiting for transfers between devices, gather_weights(): return lax.all_gather(packed, ('z', 'y'), axis=0)  68.3 us
    all_to_all x2, waiting for transfers between devices, spread(): got = lax.all_to_all(blocks, CHIPS, 0, 0, tiled=True)  64.9 us
    pallas_call x5, Pallas kernels, call(): pl.pallas_call(kernel, out_shape=[jax.ShapeDtypeStruct(shape, kind) for s...  54.3 us
    all_to_all x1, blocking collectives, local(): lax.all_to_all(jnp.concatenate([small_grads, small_grads]), CHIPS, 0, 0,...  18.9 us
    ppermute x15, starting transfers between devices, core_swap(): return lax.ppermute(value, 'c', SWAP)  17.1 us
    ppermute x9, waiting for transfers between devices, ring_shift(): return lax.ppermute(value, RING, pairs)  14.4 us
    all_to_all x2, starting transfers between devices, spread(): got = lax.all_to_all(blocks, CHIPS, 0, 0, tiled=True)  13 us
    unnamed x49, local copies, waits for them, and re-layouts  9.91 us
  transfers between devices with their start and end apart: 30, of which 12 were waited for; matrix products, arithmetic and copies ran while one was open for 12% of the time, Pallas kernels for 5%

profile of v2, /device:TPU:1, one launch (start us, length us, event | category | flops | bytes accessed | tf_op | source)
XLA Modules:
  0.0 351.8 jit_solution(4018978350286896418)
XLA Ops:
  19.1 2.6 collective-permute-start.7
  23.7 4.2 %collective-permute-done.5 = bf16[24,3200]{1,0:T(8,128)(2,1)S(1)} collective-permute-done((bf16[24,3200]{1,0:T(8,128)(2,1)S(1)}, bf16[24,3200]{1,0:T(8,128)(2,1)S(1)}, u32[]{:S(2)}, u32[]{:S(2)}) %collective-permute-start.5) | collective-permute-done | bytes 153632 | tf_op jit(solution)/shard_map/ppermute | solution.py:32
  28.9 68.3 %all-gather.3.cloned.1.call-done = bf16[768,4736]{1,0:T(8,128)(2,1)} async-done(((bf16[48,4736]{1,0:T(8,128)(2,1)}), bf16[768,4736]{1,0:T(8,128)(2,1)}) %all-gather.3.cloned.1.call-update) | async-done | bytes 7274512 | tf_op jit(solution)/shard_map/all_gather | solution.py:357
  97.2 4.9 %slice.174 = bf16[16,48,3072]{2,1,0:T(8,128)(2,1)} slice(bf16[16,48,4736]{2,1,0:T(8,128)(2,1)} %bitcast.84), slice={[0:16], [0:48], [1536:4608]} | slice | bytes 9437184 | tf_op jit(solution)/shard_map/slice | solution.py:403
  102.7 3.2 slice.172
  106.0 2.4 collective-permute-start.2
  109.6 3.4 collective-permute-done.2
  112.9 2.7 collective-permute-done.1
  115.6 5.3 %collective-permute-done = bf16[128,768]{1,0:T(8,128)(2,1)S(1)} collective-permute-done((bf16[128,768]{1,0:T(8,128)(2,1)S(1)}, bf16[128,768]{1,0:T(8,128)(2,1)S(1)}, u32[]{:S(2)}, u32[]{:S(2)}) %collective-permute-start) | collective-permute-done | bytes 196640 | tf_op jit(solution)/shard_map/ppermute | solution.py:27
  126.3 2.1 constant_dynamic-update-slice_fusion.tok
  132.6 13.5 %shard_map.262 = (bf16[1024,768]{1,0:T(8,128)(2,1)}, bf16[128,768]{1,0:T(8,128)(2,1)}, bf16[1024,768]{1,0:T(8,128)(2,1)}, bf16[1024,768]{1,0:T(8,128)(2,1)}, bf1...) custom-call(s32[8]{0:T(128)} %stack.138.meta, ...), custom_call_target="tpu_custom_call" | custom-call | flops 4000000000 | bytes 20000000 | tf_op jit(solution)/shard_map/pallas_call | solution.py:84
  146.1 12.8 %shard_map.263 = (bf16[128,768]{1,0:T(8,128)(2,1)}, bf16[128,3072]{1,0:T(8,128)(2,1)}, bf16[128,1536]{1,0:T(8,128)(2,1)}, bf16[128,1536]{1,0:T(8,128)(2,1)}, bf1...) custom-call(s32[8]{0:T(128)} %stack.138.meta, ...), custom_call_target="tpu_custom_call" | custom-call | flops 3000000000 | bytes 20000000 | tf_op jit(solution)/shard_map/pallas_call | solution.py:84
  158.9 10.3 %shard_map.264 = (bf16[128,768]{1,0:T(8,128)(2,1)}, bf16[1024,768]{1,0:T(8,128)(2,1)}, bf16[1024,768]{1,0:T(8,128)(2,1)}, f32[1,768]{1,0:T(1,128)}) custom-call(s32[8]{0:T(128)} %stack.138.meta, bf16[128,768]{1,0:T(8,128)(2,1)} %get-tuple-element.43.q, bf16[1024,768]{1,0:T(8,128)(2,1)} %get-tuple-element.44.k, bf16[1024,768]{1,0:T(8,128)(2,1)} %get-tuple-element.45.v, ...), custom_call_target="tpu_custom_call" | custom-call | flops 3000000000 | bytes 20000000 | tf_op jit(solution)/shard_map/pallas_call | solution.py:84
  170.3 3.4 collective-permute-done.11
  175.8 11.9 %shard_map.265 = (bf16[64,48,384]{2,1,0:T(8,128)(2,1)}, f32[4,128,768]{2,1,0:T(8,128)}, bf16[4,128,768]{2,1,0:T(8,128)(2,1)}) custom-call(s32[8]{0:T(128)} %stack.138.meta, bf16[1024,768]{1,0:T(8,128)(2,1)} %get-tuple-element.42.h1, bf16[1024,768]{1,0:T(8,128)(2,1)} %get-tuple-element.48.keep, bf16[1024,768]{1,0:T(8,128)(2,1)} %copy-done.2, ...), custom_call_target="tpu_custom_call" | custom-call | flops 3000000000 | bytes 20000000 | tf_op jit(solution)/shard_map/pallas_call | solution.py:84
  192.2 1.8 fusion.24
  201.2 1.6 copy.144
  203.4 2.4 collective-permute-done.15
  207.5 2.3 concatenate.78
  210.0 18.9 %all_to_all.15 = f32[64,8,256]{2,1,0:T(8,128)S(1)} all-to-all(f32[64,8,256]{2,1,0:T(8,128)S(1)} %pad_maximum_fusion.2), channel_id=1, replica_groups=mesh['xl'=2,'z'=4,'y'=4,'xh'=2,'c'=2] {'xl','z','y','xh'}, dimensions={0} | all-to-all | bytes 1048576 | tf_op jit(solution)/shard_map/all_to_all | solution.py:558
  228.9 4.7 %all-to-all-start.2 = ((bf16[64,48,384]{2,1,0:T(8,128)(2,1)}), bf16[64,48,384]{2,1,0:T(8,128)(2,1)S(1)}, u32[]{:S(2)}, u32[]{:S(2)}) async-start(bf16[64,48,384]{2,1,0:T(8,128)(2,1)} %get-tuple-element.62), calls=%async_computation.2 | async-start | bytes 4718592 | tf_op jit(solution)/shard_map/all_to_all | solution.py:361
  233.6 3.2 collective-permute-start.19
  241.2 5.8 %shard_map.266 = bf16[64,96,384]{2,1,0:T(8,128)(2,1)} custom-call(bf16[128,768]{1,0:T(8,128)(2,1)} %get-tuple-element.51.h2, bf16[128,768]{1,0:T(8,128)(2,1)} %get-tuple-element.81.h2_far, bf16[128,1536]{1,0:T(8,128)(2,1)} %get-tuple-element.59.du, bf16[128,1536]{1,0:T(8,128)(2,1)} %copy-done.10, bf16[128,3072]{1,0:T(8,128)(2,1)} %get-tuple-element.61.act, ...), custom_call_target="tpu_custom_call" | custom-call | flops 2000000000 | bytes 10000000 | tf_op jit(solution)/shard_map/pallas_call | solution.py:84
  246.9 15.2 %all-to-all-done.2 = bf16[64,48,384]{2,1,0:T(8,128)(2,1)S(1)} async-done(((bf16[64,48,384]{2,1,0:T(8,128)(2,1)}), bf16[64,48,384]{2,1,0:T(8,128)(2,1)S(1)}, u32[]{:S(2)}, u32[]{:S(2)}) %all-to-all-start.2) | async-done | bytes 2359328 | tf_op jit(solution)/shard_map/all_to_all | solution.py:361
  262.1 8.3 %all-to-all-start.1 = ((bf16[64,96,384]{2,1,0:T(8,128)(2,1)}), bf16[64,96,384]{2,1,0:T(8,128)(2,1)}, u32[]{:S(2)}, u32[]{:S(2)}) async-start(bf16[64,96,384]{2,1,0:T(8,128)(2,1)} %shard_map.266), calls=%async_computation.1 | async-start | bytes 9437184 | tf_op jit(solution)/shard_map/all_to_all | solution.py:361
  270.6 2.0 collective-permute-start.17
  272.6 1.9 fusion.15
  274.9 49.8 %all-to-all-done.1 = bf16[64,96,384]{2,1,0:T(8,128)(2,1)} async-done(((bf16[64,96,384]{2,1,0:T(8,128)(2,1)}), bf16[64,96,384]{2,1,0:T(8,128)(2,1)}, u32[]{:S(2)}, u32[]{:S(2)}) %all-to-all-start.1) | async-done | bytes 4718624 | tf_op jit(solution)/shard_map/all_to_all | solution.py:361
  324.7 3.0 reduce
  328.4 2.7 collective-permute-start.22
  332.8 5.0 %collective-permute-start.25 = (bf16[48,384]{1,0:T(8,128)(2,1)S(1)}, bf16[48,384]{1,0:T(8,128)(2,1)S(1)}, u32[]{:S(2)}, u32[]{:S(2)}) collective-permute-start(bf16[48,384]{1,0:T(8,128)(2,1)S(1)} %get-tuple-element.98), channel_id=1, source_target_pairs={{0,1},{1,0},{2,3},{3,2},{4,5},{5,4},{6,7},{7,6},{8,9},{9,8},{10,11... | collective-permute-start | bytes 110600 | tf_op jit(solution)/shard_map/ppermute | solution.py:36
  338.2 1.8 collective-permute-start.24
  (169 shorter events, 55.6 us)
Async XLA Ops:
  7.2 90.0 %all-gather.3.cloned.1.call-start = ((), (), s32[]{:S(2)}) async-start(), calls=%async_computation.3 | async-start | bytes 7729152 | tf_op jit(solution)/shard_map/all_gather | solution.py:357
  8.0 11.1 %collective-permute-start.6 = (bf16[48,384]{1,0:T(8,128)(2,1)S(1)}, bf16[48,384]{1,0:T(8,128)(2,1)S(1)}, u32[]{:S(2)}, u32[]{:S(2)}) collective-permute-start(bf16[48,384]{1,0:T(8,128)(2,1)S(1)} %get-tuple-element.105), channel_id=1, source_target_pairs={{0,1},{1,0},{2,3},{3,2},{4,5},{5,4},{6,7},{7,6},{8,9},{9,8},{10,11... | collective-permute-start | bytes 110600 | tf_op jit(solution)/shard_map/ppermute | solution.py:36
  18.9 2.9 collective-permute-start.4
  19.1 4.5 %collective-permute-start.7 = (bf16[96,384]{1,0:T(8,128)(2,1)S(1)}, bf16[96,384]{1,0:T(8,128)(2,1)S(1)}, u32[]{:S(2)}, u32[]{:S(2)}) collective-permute-start(bf16[96,384]{1,0:T(8,128)(2,1)S(1)} %maximum_select_fusion.3), channel_id=1, source_target_pairs={{0,66},{64,2},{2,64},{66,0},{1,67},{65,3},{3,65},{67,1},{4,70},{68... | collective-permute-start | bytes 221192 | tf_op jit(solution)/shard_map/ppermute | solution.py:32
  21.9 6.0 %collective-permute-start.5 = (bf16[24,3200]{1,0:T(8,128)(2,1)S(1)}, bf16[24,3200]{1,0:T(8,128)(2,1)S(1)}, u32[]{:S(2)}, u32[]{:S(2)}) collective-permute-start(bf16[24,3200]{1,0:T(8,128)(2,1)S(1)} %maximum_select_fusion.1), channel_id=1, source_target_pairs={{0,66},{64,2},{2,64},{66,0},{1,67},{65,3},{3,65},{67,1},{4,70},{68... | collective-permute-start | bytes 460808 | tf_op jit(solution)/shard_map/ppermute | solution.py:32
  102.0 44.1 %collective-permute-start.9 = (bf16[16,48,3072]{2,1,0:T(8,128)(2,1)}, bf16[16,48,3072]{2,1,0:T(8,128)(2,1)}, u32[]{:S(2)}, u32[]{:S(2)}) collective-permute-start(bf16[16,48,3072]{2,1,0:T(8,128)(2,1)} %slice.174), channel_id=1, source_target_pairs={{0,1},{1,0},{2,3},{3,2},{4,5},{5,4},{6,7},{7,6},{8,9},{9,8},{10,11... | collective-permute-start | bytes 14155784 | tf_op jit(solution)/shard_map/ppermute | solution.py:36
  106.0 25.2 %collective-permute-start.8 = (bf16[16,48,1536]{2,1,0:T(8,128)(2,1)}, bf16[16,48,1536]{2,1,0:T(8,128)(2,1)S(1)}, u32[]{:S(2)}, u32[]{:S(2)}) collective-permute-start(bf16[16,48,1536]{2,1,0:T(8,128)(2,1)} %slice.172), channel_id=1, source_target_pairs={{0,1},{1,0},{2,3},{3,2},{4,5},{5,4},{6,7},{7,6},{8,9},{9,8},{10,11... | collective-permute-start | bytes 7077896 | tf_op jit(solution)/shard_map/ppermute | solution.py:36
  106.0 6.9 %collective-permute-start.2 = (bf16[128,768]{1,0:T(8,128)(2,1)S(1)}, bf16[128,768]{1,0:T(8,128)(2,1)S(1)}, u32[]{:S(2)}, u32[]{:S(2)}) collective-permute-start(bf16[128,768]{1,0:T(8,128)(2,1)S(1)} %bitcast.90), channel_id=1, source_target_pairs={{0,66},{64,0},{2,64},{66,2},{1,67},{65,1},{3,65},{67,3},{4,70},{68... | collective-permute-start | bytes 589832 | tf_op jit(solution)/shard_map/ppermute | solution.py:27
  108.4 7.2 %collective-permute-start.1 = (bf16[128,768]{1,0:T(8,128)(2,1)S(1)}, bf16[128,768]{1,0:T(8,128)(2,1)S(1)}, u32[]{:S(2)}, u32[]{:S(2)}) collective-permute-start(bf16[128,768]{1,0:T(8,128)(2,1)S(1)} %bitcast.91), channel_id=1, source_target_pairs={{0,2},{64,66},{2,0},{66,64},{1,3},{65,67},{3,1},{67,65},{4,6},{68,... | collective-permute-start | bytes 589832 | tf_op jit(solution)/shard_map/ppermute | solution.py:27
  109.0 12.0 %collective-permute-start = (bf16[128,768]{1,0:T(8,128)(2,1)S(1)}, bf16[128,768]{1,0:T(8,128)(2,1)S(1)}, u32[]{:S(2)}, u32[]{:S(2)}) collective-permute-start(bf16[128,768]{1,0:T(8,128)(2,1)S(1)} %bitcast.92), channel_id=1, source_target_pairs={{0,64},{64,2},{2,66},{66,0},{1,65},{65,3},{3,67},{67,1},{4,68},{68... | collective-permute-start | bytes 589832 | tf_op jit(solution)/shard_map/ppermute | solution.py:27
  121.9 4.4 %collective-permute-start.3 = (bf16[4,128,768]{2,1,0:T(8,128)(2,1)}, bf16[4,128,768]{2,1,0:T(8,128)(2,1)}, u32[]{:S(2)}, u32[]{:S(2)}) collective-permute-start(bf16[4,128,768]{2,1,0:T(8,128)(2,1)} %pad_maximum_fusion), channel_id=1, source_target_pairs={{0,1},{1,0},{2,3},{3,2},{4,5},{5,4},{6,7},{7,6},{8,9},{9,8},{10,11... | collective-permute-start | bytes 2359304 | tf_op jit(solution)/shard_map/ppermute | solution.py:36
  169.2 5.4 %collective-permute-start.10 = (bf16[1024,768]{1,0:T(8,128)(2,1)}, bf16[1024,768]{1,0:T(8,128)(2,1)S(1)}, u32[]{:S(2)}, u32[]{:S(2)}) collective-permute-start(bf16[1024,768]{1,0:T(8,128)(2,1)} %get-tuple-element.49), channel_id=1, source_target_pairs={{0,1},{1,0},{2,3},{3,2},{4,5},{5,4},{6,7},{7,6},{8,9},{9,8},{10,11... | collective-permute-start | bytes 4718600 | tf_op jit(solution)/shard_map/ppermute | solution.py:36
  169.3 4.4 %collective-permute-start.11 = (bf16[384,768]{1,0:T(8,128)(2,1)S(1)}, bf16[384,768]{1,0:T(8,128)(2,1)S(1)}, u32[]{:S(2)}, u32[]{:S(2)}) collective-permute-start(bf16[384,768]{1,0:T(8,128)(2,1)S(1)} %pad_maximum_fusion.1), channel_id=1, source_target_pairs={{0,1},{1,0},{2,3},{3,2},{4,5},{5,4},{6,7},{7,6},{8,9},{9,8},{10,11... | collective-permute-start | bytes 1769480 | tf_op jit(solution)/shard_map/ppermute | solution.py:36
  170.0 4.6 %collective-permute-start.12 = (bf16[128,768]{1,0:T(8,128)(2,1)}, bf16[128,768]{1,0:T(8,128)(2,1)S(1)}, u32[]{:S(2)}, u32[]{:S(2)}) collective-permute-start(bf16[128,768]{1,0:T(8,128)(2,1)} %get-tuple-element.53.dq), channel_id=1, source_target_pairs={{0,1},{1,0},{2,3},{3,2},{4,5},{5,4},{6,7},{7,6},{8,9},{9,8},{10,11... | collective-permute-start | bytes 589832 | tf_op jit(solution)/shard_map/ppermute | solution.py:36
  187.8 3.5 %collective-permute-start.13 = (bf16[4,128,768]{2,1,0:T(8,128)(2,1)}, bf16[4,128,768]{2,1,0:T(8,128)(2,1)S(1)}, u32[]{:S(2)}, u32[]{:S(2)}) collective-permute-start(bf16[4,128,768]{2,1,0:T(8,128)(2,1)} %get-tuple-element.55), channel_id=1, source_target_pairs={{0,1},{1,0},{2,3},{3,2},{4,5},{5,4},{6,7},{7,6},{8,9},{9,8},{10,11... | collective-permute-start | bytes 2359304 | tf_op jit(solution)/shard_map/ppermute | solution.py:36
  194.8 8.0 %collective-permute-start.14 = (bf16[128,768]{1,0:T(8,128)(2,1)}, bf16[128,768]{1,0:T(8,128)(2,1)S(1)}, u32[]{:S(2)}, u32[]{:S(2)}) collective-permute-start(bf16[128,768]{1,0:T(8,128)(2,1)} %get-tuple-element.78), channel_id=1, source_target_pairs={{0,66},{64,0},{2,64},{66,2},{1,67},{65,1},{3,65},{67,3},{4,70},{68... | collective-permute-start | bytes 589832 | tf_op jit(solution)/shard_map/ppermute | solution.py:27
  195.2 8.2 %collective-permute-start.16 = (bf16[128,768]{1,0:T(8,128)(2,1)}, bf16[128,768]{1,0:T(8,128)(2,1)S(1)}, u32[]{:S(2)}, u32[]{:S(2)}) collective-permute-start(bf16[128,768]{1,0:T(8,128)(2,1)} %get-tuple-element.79), channel_id=1, source_target_pairs={{0,64},{64,2},{2,66},{66,0},{1,65},{65,3},{3,67},{67,1},{4,68},{68... | collective-permute-start | bytes 589832 | tf_op jit(solution)/shard_map/ppermute | solution.py:27
  196.3 9.5 %collective-permute-start.15 = (bf16[128,768]{1,0:T(8,128)(2,1)S(1)}, bf16[128,768]{1,0:T(8,128)(2,1)}, u32[]{:S(2)}, u32[]{:S(2)}) collective-permute-start(bf16[128,768]{1,0:T(8,128)(2,1)S(1)} %get-tuple-element.80), channel_id=1, source_target_pairs={{0,2},{64,66},{2,0},{66,64},{1,3},{65,67},{3,1},{67,65},{4,6},{68,... | collective-permute-start | bytes 589832 | tf_op jit(solution)/shard_map/ppermute | solution.py:27
  228.9 33.2 %all-to-all-start.2 = ((bf16[64,48,384]{2,1,0:T(8,128)(2,1)}), bf16[64,48,384]{2,1,0:T(8,128)(2,1)S(1)}, u32[]{:S(2)}, u32[]{:S(2)}) async-start(bf16[64,48,384]{2,1,0:T(8,128)(2,1)} %get-tuple-element.62), calls=%async_computation.2 | async-start | bytes 4718592 | tf_op jit(solution)/shard_map/all_to_all | solution.py:361
  233.6 6.5 %collective-permute-start.19 = (bf16[128,3072]{1,0:T(8,128)(2,1)}, bf16[128,3072]{1,0:T(8,128)(2,1)S(1)}, u32[]{:S(2)}, u32[]{:S(2)}) collective-permute-start(bf16[128,3072]{1,0:T(8,128)(2,1)} %get-tuple-element.61.act), channel_id=1, source_target_pairs={{0,1},{1,0},{2,3},{3,2},{4,5},{5,4},{6,7},{7,6},{8,9},{9,8},{10,11... | collective-permute-start | bytes 2359304 | tf_op jit(solution)/shard_map/ppermute | solution.py:36
  236.8 3.3 collective-permute-start.18
  238.5 1.6 collective-permute-start.20
  246.9 25.7 %copy-start.17 = (f32[128]{0:T(128)S(1)}, f32[128]{0:T(128)}, u32[]{:S(2)}) copy-start(f32[128]{0:T(128)} %copy-done.16) | copy-start | bytes 1540
  246.9 25.7 %copy-start.18 = (f32[128]{0:T(128)S(1)}, f32[128]{0:T(128)}, u32[]{:S(2)}) copy-start(f32[128]{0:T(128)} %add_rsqrt_fusion) | copy-start | bytes 1540
  262.1 62.6 %all-to-all-start.1 = ((bf16[64,96,384]{2,1,0:T(8,128)(2,1)}), bf16[64,96,384]{2,1,0:T(8,128)(2,1)}, u32[]{:S(2)}, u32[]{:S(2)}) async-start(bf16[64,96,384]{2,1,0:T(8,128)(2,1)} %shard_map.266), calls=%async_computation.1 | async-start | bytes 9437184 | tf_op jit(solution)/shard_map/all_to_all | solution.py:361
  270.6 3.8 %collective-permute-start.17 = (f32[8,256]{1,0:T(8,128)S(1)}, f32[8,256]{1,0:T(8,128)S(1)}, u32[]{:S(2)}, u32[]{:S(2)}) collective-permute-start(f32[8,256]{1,0:T(8,128)S(1)} %reduce_sum.97), channel_id=1, source_target_pairs={{0,1},{1,0},{2,3},{3,2},{4,5},{5,4},{6,7},{7,6},{8,9},{9,8},{10,11... | collective-permute-start | bytes 24584 | tf_op jit(solution)/shard_map/ppermute | solution.py:36
  327.7 10.1 %collective-permute-start.21 = (bf16[2,24,384]{2,1,0:T(8,128)(2,1)S(1)}, bf16[2,24,384]{2,1,0:T(8,128)(2,1)S(1)}, u32[]{:S(2)}, u32[]{:S(2)}) collective-permute-start(bf16[2,24,384]{2,1,0:T(8,128)(2,1)S(1)} %get-tuple-element.101), channel_id=1, source_target_pairs={{0,64},{64,2},{2,66},{66,0},{1,65},{65,3},{3,67},{67,1},{4,68},{68... | collective-permute-start | bytes 110600 | tf_op jit(solution)/shard_map/ppermute | solution.py:27
  328.4 9.5 %collective-permute-start.22 = (bf16[2,24,384]{2,1,0:T(8,128)(2,1)S(1)}, bf16[2,24,384]{2,1,0:T(8,128)(2,1)S(1)}, u32[]{:S(2)}, u32[]{:S(2)}) collective-permute-start(bf16[2,24,384]{2,1,0:T(8,128)(2,1)S(1)} %get-tuple-element.102), channel_id=1, source_target_pairs={{0,2},{64,66},{2,0},{66,64},{1,3},{65,67},{3,1},{67,65},{4,6},{68,... | collective-permute-start | bytes 110600 | tf_op jit(solution)/shard_map/ppermute | solution.py:27
  331.1 6.8 %collective-permute-start.23 = (bf16[2,24,384]{2,1,0:T(8,128)(2,1)S(1)}, bf16[2,24,384]{2,1,0:T(8,128)(2,1)S(1)}, u32[]{:S(2)}, u32[]{:S(2)}) collective-permute-start(bf16[2,24,384]{2,1,0:T(8,128)(2,1)S(1)} %get-tuple-element.103), channel_id=1, source_target_pairs={{0,66},{64,0},{2,64},{66,2},{1,67},{65,1},{3,65},{67,3},{4,70},{68... | collective-permute-start | bytes 110600 | tf_op jit(solution)/shard_map/ppermute | solution.py:27
  332.8 7.1 %collective-permute-start.25 = (bf16[48,384]{1,0:T(8,128)(2,1)S(1)}, bf16[48,384]{1,0:T(8,128)(2,1)S(1)}, u32[]{:S(2)}, u32[]{:S(2)}) collective-permute-start(bf16[48,384]{1,0:T(8,128)(2,1)S(1)} %get-tuple-element.98), channel_id=1, source_target_pairs={{0,1},{1,0},{2,3},{3,2},{4,5},{5,4},{6,7},{7,6},{8,9},{9,8},{10,11... | collective-permute-start | bytes 110600 | tf_op jit(solution)/shard_map/ppermute | solution.py:36
  338.2 3.2 collective-permute-start.24
  340.0 4.1 %collective-permute-start.26 = (bf16[48,768]{1,0:T(8,128)(2,1)S(1)}, bf16[48,768]{1,0:T(8,128)(2,1)S(1)}, u32[]{:S(2)}, u32[]{:S(2)}) collective-permute-start(bf16[48,768]{1,0:T(8,128)(2,1)S(1)} %maximum_select_fusion.4), channel_id=1, source_target_pairs={{0,64},{64,0},{1,65},{65,1},{2,66},{66,2},{3,67},{67,3},{4,68},{68... | collective-permute-start | bytes 221192 | tf_op jit(solution)/shard_map/ppermute | solution.py:565
  (17 other events, 80.6 us)
Sparse Core Ops, SparseCore 0:
  29.0 68.1 all-gather.2
